TPU v7x, 128 devices: a whole 4x4x4 slice. The times are simulated.
128 devices in a mesh: dp: 16 (over z, y), expert: 8 (over x, core).
Axes of the slice: x: 4, y: 4, z: 4, core: 2. Of those that a mesh axis runs over, the one named last changes fastest.
Arguments:
- residual: bfloat16 [8192, 5120], P('dp', 'expert'), may hold values from -36 to 36
- queries: bfloat16 [8192, 5120], P('dp', 'expert'), may hold values from -6 to 6
- keys: bfloat16 [8192, 1024], P('dp', 'expert'), may hold values from -6 to 6
- values: bfloat16 [8192, 1024], P('dp', 'expert'), may hold values from -6 to 6
- lengths: int32 [16, 8], replicated, may hold values from 2 to 256, as said below
- w_out: bfloat16 [5120, 5120], P('expert'), may hold values from -0.125 to 0.125
- w_router: bfloat16 [5120, 16], replicated, may hold values from -0.078125 to 0.078125
- expert_ids: int32 [8192], P('dp'), may hold values from 0 to 15, as said below
- w_gate: bfloat16 [16, 5120, 4096], P('dp', None, 'expert'), may hold values from -0.078125 to 0.078125
- w_up: bfloat16 [16, 5120, 4096], P('dp', None, 'expert'), may hold values from -0.078125 to 0.078125
- w_down: bfloat16 [16, 4096, 5120], P('dp', 'expert'), may hold values from -0.5 to 0.5
Outputs:
- attended: bfloat16 [8192, 5120], P('dp', 'expert')
- expert_out: bfloat16 [8192, 5120], P('dp', 'expert')
Inputs may be any that keep to these rules, and one draw needn't show every extreme that they name: `lengths`: each row sums to 512; every document has 2 or more tokens, and each row has one document of exactly 256 tokens. `expert_ids`: within each sequence of 512 tokens no expert is chosen by more than 48 tokens; in every draw one expert is chosen by exactly 48 tokens of every sequence.
All inputs are finite; a program needn't handle non-finite values.
Results may differ from a plain program's by a relative error of at most 0.038.
Values may be sent and summed in bfloat16 or wider, within the bound.
No kernel may reach another device: no remote copies, remote signals or barrier semaphores. Data moves between devices by JAX's collectives and lax.ppermute only.
A program may use at most 128 MiB of HBM per device.

v0:
```python
import math

import jax
import jax.numpy as jnp
from jax import lax
from jax.sharding import PartitionSpec as P

HD = 128


epsilon = 1e-05


def doc_ids(length_row, positions):
    bounds = jnp.cumsum(length_row)
    return jnp.sum((positions[:, None] >= bounds[None, :]).astype(jnp.int32), axis=1)


def attend_local(seq_queries, seq_keys, seq_values, length_row):
    seq_len = seq_queries.shape[0]
    head_width = seq_queries.shape[1]
    kv_local = seq_keys.shape[1] // HD
    group_size = head_width // HD // kv_local
    positions = jnp.arange(seq_len, dtype=jnp.int32)
    documents = doc_ids(length_row, positions)
    allowed = (documents[:, None] == documents[None, :]) & (
        positions[None, :] <= positions[:, None]
    )
    shaped_q = seq_queries.reshape(seq_len, kv_local, group_size, HD)
    shaped_k = seq_keys.reshape(seq_len, kv_local, HD)
    shaped_v = seq_values.reshape(seq_len, kv_local, HD)
    scores = jnp.einsum(
        "qkgd,skd->kgqs", shaped_q, shaped_k, preferred_element_type=jnp.float32
    ) / math.sqrt(HD)
    masked = jnp.where(allowed[None, None], scores, -1e30)
    row_max = jnp.max(masked, axis=-1, keepdims=True)
    raised = jnp.exp(masked - row_max)
    weights = (raised / jnp.sum(raised, axis=-1, keepdims=True)).astype(jnp.bfloat16)
    mixture = jnp.einsum("kgqs,skd->qkgd", weights, shaped_v, preferred_element_type=jnp.float32)
    return mixture.astype(jnp.bfloat16).reshape(seq_len, head_width)


def shards(
    residual, queries, keys, values, lengths, w_out, w_router, expert_ids, w_gate, w_up, w_down
):
    seq_len = queries.shape[0]
    dp_count = lax.axis_size("dp")
    row_index = lax.axis_index("dp")
    device_slots = jnp.arange(dp_count, dtype=jnp.int32)
    own_lengths = jnp.sum(jnp.where((device_slots == row_index)[:, None], lengths, 0), axis=0)
    context = attend_local(queries, keys, values, own_lengths)
    slice_width = residual.shape[1]
    column_start = lax.axis_index("expert") * slice_width
    projected = jnp.dot(context, w_out, preferred_element_type=jnp.float32)
    own_part = lax.dynamic_slice_in_dim(projected, column_start, slice_width, 1) + residual.astype(
        jnp.float32
    )
    projected = lax.dynamic_update_slice_in_dim(projected, own_part, column_start, 1)
    expert_count = w_router.shape[1]
    expert_slots = jnp.arange(expert_count, dtype=jnp.int32)
    onehot = expert_ids[:, None] == expert_slots[None, :]
    capacity = 3 * seq_len // (2 * expert_count)
    counts_so_far = jnp.cumsum(onehot.astype(jnp.int32), axis=0)
    slot_rank = jnp.sum(jnp.where(onehot, counts_so_far, 0), axis=1) - 1
    slot_of_token = expert_ids * capacity + slot_rank
    total_slots = expert_count * capacity
    token_of_slot = (
        jnp.zeros((total_slots,), jnp.int32)
        .at[slot_of_token]
        .set(jnp.arange(seq_len, dtype=jnp.int32))
    )
    slot_filled = jnp.zeros((total_slots,), jnp.bool_).at[slot_of_token].set(True)
    attended_full = lax.psum(projected.astype(jnp.bfloat16), "expert")
    attended = lax.dynamic_slice_in_dim(attended_full, column_start, slice_width, 1)
    stream = attended_full.astype(jnp.float32)
    inverse_rms = lax.rsqrt(jnp.mean(stream * stream, axis=1, keepdims=True) + epsilon)
    normed = (stream * inverse_rms).astype(jnp.bfloat16)
    logits = jnp.dot(normed, w_router, preferred_element_type=jnp.float32)
    chosen = jnp.sum(jnp.where(onehot, logits, 0.0), axis=1)
    routed = (normed.astype(jnp.float32) * jax.nn.sigmoid(chosen)[:, None]).astype(jnp.bfloat16)
    model_width = routed.shape[1]
    outgoing = jnp.where(slot_filled[:, None], routed[token_of_slot], jnp.zeros((), jnp.bfloat16))
    outgoing = outgoing.reshape(dp_count, total_slots // dp_count, model_width)
    arrived = lax.all_to_all(outgoing, "dp", split_axis=0, concat_axis=0, tiled=True)
    local_experts = w_gate.shape[0]
    arrival = arrived.reshape(dp_count, local_experts, capacity, model_width)
    gate_part = jnp.einsum("nxcd,xdf->nxcf", arrival, w_gate, preferred_element_type=jnp.float32)
    up_part = jnp.einsum("nxcd,xdf->nxcf", arrival, w_up, preferred_element_type=jnp.float32)
    hidden = (jax.nn.silu(gate_part) * up_part).astype(jnp.bfloat16)
    partial_value = jnp.einsum("nxcf,xfd->nxcd", hidden, w_down, preferred_element_type=jnp.float32)
    partial_value = partial_value.reshape(dp_count, local_experts * capacity, model_width)
    returned = lax.all_to_all(
        partial_value.astype(jnp.bfloat16), "dp", split_axis=0, concat_axis=0, tiled=True
    )
    per_token = returned.reshape(total_slots, model_width)[slot_of_token].astype(jnp.float32)
    expert_out = lax.psum_scatter(
        per_token.astype(jnp.bfloat16), "expert", scatter_dimension=1, tiled=True
    )
    return (attended, expert_out)


def solution(mesh):
    in_specs = (
        P("dp", "expert"),
        P("dp", "expert"),
        P("dp", "expert"),
        P("dp", "expert"),
        P(),
        P("expert", None),
        P(),
        P("dp"),
        P("dp", None, "expert"),
        P("dp", None, "expert"),
        P("dp", "expert", None),
    )
    out_specs = (P("dp", "expert"), P("dp", "expert"))
    return jax.shard_map(shards, mesh=mesh, in_specs=in_specs, out_specs=out_specs, check_vma=False)
```

profile of v0, /device:TPU:0, one launch (start us, length us, event | category | flops | bytes accessed | tf_op | source)
XLA Modules:
  0.0 451.7 jit_solution(5777801622569526158)
XLA Ops:
  7.2 0.0 copy-start
  7.2 0.0 all-reduce.2.cloned.1.call-start
  7.2 0.8 select_reduce_fusion
  8.1 0.2 reduce-window.18
  8.3 0.1 convert_reduce_fusion
  8.3 0.2 fusion.32
  8.6 1.3 copy.27
  9.9 0.0 copy-start.5
  9.9 2.0 fusion.8
  11.9 0.0 slice-start
  11.9 1.1 fusion.7
  13.0 0.0 copy-done.5
  13.0 0.0 slice-start.1
  13.0 1.6 fusion.20
  14.6 0.5 slice-done.1
  15.1 6.8 %fusion.45 = f32[512,5120]{1,0:T(8,128)} fusion(bf16[512,640]{0,1:T(8,128)(2,1)S(1)} %bitcast.117, bf16[640,5120]{1,0:T(8,128)(2,1)S(1)} %bitcast.115), kind=kOutput, calls=%fused_computation.67 | convolution fusion | flops 3355443200 | bytes 17694720 | tf_op jit(solution)/shard_map/dot_general | solution.py:54
  21.9 2.5 add_dynamic-update-slice_fusion
  24.4 7.1 %convert_element_type.56 = bf16[512,5120]{1,0:T(8,128)(2,1)} convert(f32[512,5120]{1,0:T(8,128)} %add_dynamic-update-slice_fusion) | non-fusion elementwise | flops 2621440 | bytes 15728640 | tf_op jit(solution)/shard_map/convert_element_type | solution.py:73
  31.5 0.0 all-reduce.2.cloned.1.call-update
  31.6 0.7 copy-done.4
  32.2 1.1 reduce-window.19
  33.4 0.2 slice_reduce_fusion
  33.6 0.1 fusion.37
  33.8 2.4 scatter_custom_fusion.1
  36.2 2.6 scatter_custom_fusion
  38.9 0.1 broadcast_in_dim.83
  39.0 71.8 %all-reduce.2.cloned.1.call-done = bf16[512,5120]{1,0:T(8,128)(2,1)} async-done(((bf16[512,5120]{1,0:T(8,128)(2,1)}), bf16[512,5120]{1,0:T(8,128)(2,1)}) %all-reduce.2.cloned.1.call-update) | async-done | bytes 5242896 | tf_op jit(solution)/shard_map/psum | solution.py:73
  110.8 3.7 fusion
  114.5 0.3 copy-done.2
  114.8 1.6 fusion.29
  116.4 4.8 %multiply_convert_fusion = bf16[512,5120]{1,0:T(8,128)(2,1)} fusion(f32[512]{0:T(512)S(1)} %add_divide_fusion, f32[512]{0:T(512)S(1)} %add_rsqrt_fusion, bf16[512,5120]{1,0:T(8,128)(2,1)S(1)} %copy-done.2), kind=kLoop, calls=%fused_computation.8 | loop fusion | flops 15728640 | bytes 10489856 | tf_op jit(solution)/shard_map/convert_element_type | solution.py:80
  121.2 17.9 %gather_fusion = bf16[768,5120]{1,0:T(8,128)(2,1)} fusion(bf16[512,5120]{1,0:T(8,128)(2,1)} %multiply_convert_fusion, s32[1024]{0:T(1024)S(1)} %pad_clamp_fusion.1), kind=kCustom, calls=%fused_computation | custom fusion | bytes 15731712 | tf_op jit(solution)/shard_map/gather | solution.py:82
  139.0 3.8 broadcast_select_fusion
  142.8 0.0 slice-start.2
  142.9 96.8 %all_to_all.10 = bf16[16,48,5120]{2,1,0:T(8,128)(2,1)S(1)} all-to-all(bf16[16,48,5120]{2,1,0:T(8,128)(2,1)S(1)} %broadcast_select_fusion), channel_id=1, replica_groups=mesh['dp'=16,'expert'=8] {'dp'}, dimensions={0} | all-to-all | bytes 15728640 | tf_op jit(solution)/shard_map/all_to_all | solution.py:84
  239.7 6.5 %fusion.5 = f32[16,48,512]{2,1,0:T(8,128)S(1)} fusion(bf16[16,48,5120]{2,1,0:T(8,128)(2,1)S(1)} %all_to_all.10, bf16[1,5120,512]{2,1,0:T(8,128)(2,1)} %param.19), kind=kOutput, calls=%fused_computation.15 | convolution fusion | flops 4026531840 | bytes 14680064 | tf_op jit(solution)/shard_map/nxcd,xdf->nxcf/dot_general | solution.py:87
  246.2 0.0 slice-start.5
  246.2 4.4 fusion.23
  250.6 6.5 %convolution_convert_fusion = bf16[16,48,5120]{2,1,0:T(8,128)(2,1)} fusion(bf16[16,48,512]{2,1,0:T(8,128)(2,1)S(1)} %fusion.23, bf16[1,512,5120]{2,1,0:T(8,128)(2,1)S(1)} %bitcast.125), kind=kOutput, calls=%fused_computation.9 | convolution fusion | flops 4030464000 | bytes 13893632 | tf_op jit(solution)/shard_map/nxcf,xfd->nxcd/dot_general | solution.py:90
  257.2 4.7 %all-to-all-start.1 = ((bf16[16,48,5120]{2,1,0:T(8,128)(2,1)}), bf16[16,48,5120]{2,1,0:T(8,128)(2,1)}, u32[]{:S(2)}, u32[]{:S(2)}) async-start(bf16[16,48,5120]{2,1,0:T(8,128)(2,1)} %convolution_convert_fusion), calls=%async_computation.1 | async-start | bytes 15728640 | tf_op jit(solution)/shard_map/all_to_all | solution.py:92
  261.9 0.3 reduce-scatter.4.cloned.1.call-start
  262.2 113.7 %all-to-all-done.1 = bf16[16,48,5120]{2,1,0:T(8,128)(2,1)} async-done(((bf16[16,48,5120]{2,1,0:T(8,128)(2,1)}), bf16[16,48,5120]{2,1,0:T(8,128)(2,1)}, u32[]{:S(2)}, u32[]{:S(2)}) %all-to-all-start.1) | async-done | bytes 7864352 | tf_op jit(solution)/shard_map/all_to_all | solution.py:92
  375.9 14.7 %gather_fusion.1 = bf16[512,5120]{1,0:T(8,128)(2,1)} fusion(bf16[768,5120]{1,0:T(8,128)(2,1)} %bitcast.30, s32[1024]{0:T(1024)S(1)} %pad_clamp_fusion), kind=kCustom, calls=%fused_computation.1 | custom fusion | bytes 10487808 | tf_op jit(solution)/shard_map/gather | solution.py:95
  390.6 8.0 %copy.36 = bf16[512,5120]{0,1:T(8,128)(2,1)} copy(bf16[512,5120]{1,0:T(8,128)(2,1)} %gather_fusion.1) | data formatting | bytes 10485760
  398.6 0.0 reduce-scatter.4.cloned.1.call-update
  398.6 2.0 constant_dynamic-slice_fusion
  400.6 42.1 %reduce-scatter.4.cloned.1.call-done = bf16[640,512]{1,0:T(8,128)(2,1)} async-done(((bf16[5120,512]{1,0:T(8,128)(2,1)}), bf16[640,512]{1,0:T(8,128)(2,1)}) %reduce-scatter.4.cloned.1.call-update) | async-done | bytes 655376
  442.7 2.2 copy.37
  (29 shorter events, 0.1 us)
Async XLA Ops:
  7.2 107.3 %copy-start = (bf16[5120,16]{0,1:T(8,128)(2,1)S(1)}, bf16[5120,16]{0,1:T(8,128)(2,1)}, u32[]{:S(2)}) copy-start(bf16[5120,16]{0,1:T(8,128)(2,1)} %param.17) | copy-start | bytes 491524
  7.2 103.6 %all-reduce.2.cloned.1.call-start = ((), (), s32[]{:S(2)}) async-start(), calls=%async_computation.3 | async-start | bytes 10485760 | tf_op jit(solution)/shard_map/psum | solution.py:73
  9.9 3.1 copy-start.5
  11.9 2.7 slice-start
  13.0 2.0 slice-start.1
  15.1 6.8 %copy-start.3 = (bf16[512,640]{1,0:T(8,128)(2,1)S(1)}, bf16[512,640]{1,0:T(8,128)(2,1)}, u32[]{:S(2)}) copy-start(bf16[512,640]{1,0:T(8,128)(2,1)} %param.11) | copy-start | bytes 1966084
  31.5 0.7 copy-start.4
  110.8 4.0 copy-start.2
  142.8 103.3 %slice-start.2 = ((s8[5242880]{0:T(1024)(128)(4,1)}), s8[4194304]{0:T(1024)(128)(4,1)S(1)}, s32[]{:S(2)}) async-start(s8[5242880]{0:T(1024)(128)(4,1)} %bitcast.122), calls=%async_computation.7 | async-start | bytes 8388608
  239.7 6.5 %slice-start.3 = ((s8[5242880]{0:T(1024)(128)(4,1)}), s8[1048576]{0:T(1024)(128)(4,1)S(1)}, s32[]{:S(2)}) async-start(s8[5242880]{0:T(1024)(128)(4,1)} %bitcast.122), calls=%async_computation.8 | async-start | bytes 2097152
  239.7 10.9 %slice-start.4 = ((s8[5242880]{0:T(1024)(128)(4,1)}), s8[4194304]{0:T(1024)(128)(4,1)S(1)}, s32[]{:S(2)}) async-start(s8[5242880]{0:T(1024)(128)(4,1)} %bitcast.124), calls=%async_computation.9 | async-start | bytes 8388608
  246.2 4.4 slice-start.5
  257.2 118.8 %all-to-all-start.1 = ((bf16[16,48,5120]{2,1,0:T(8,128)(2,1)}), bf16[16,48,5120]{2,1,0:T(8,128)(2,1)}, u32[]{:S(2)}, u32[]{:S(2)}) async-start(bf16[16,48,5120]{2,1,0:T(8,128)(2,1)} %convolution_convert_fusion), calls=%async_computation.1 | async-start | bytes 15728640 | tf_op jit(solution)/shard_map/all_to_all | solution.py:92
  261.9 180.9 %reduce-scatter.4.cloned.1.call-start = ((), (), s32[]{:S(2)}) async-start(), calls=%async_computation.4 | async-start | bytes 5898240
  390.6 54.3 %copy-start.1 = (bf16[5120,16]{0,1:T(8,128)(2,1)S(1)}, bf16[5120,16]{0,1:T(8,128)(2,1)}, u32[]{:S(2)}) copy-start(bf16[5120,16]{0,1:T(8,128)(2,1)} %param.17) | copy-start | bytes 491524
Sparse Core Ops, SparseCore 0:
  31.7 79.0 all-reduce.1
  398.8 43.9 reduce-scatter.3
where the time goes:
time: 453 us; the launch traced here: 452 us
  waiting for transfers between devices  228 us (50%)
  blocking collectives  96.8 us (21%)
  local copies, waits for them, and re-layouts  52.9 us (12%)
  matrix products  29.3 us (6%)
  other arithmetic  25.7 us (6%)
  between operations  14.3 us (3%)
  starting transfers between devices  5.04 us (1%)
    all_to_all x1, waiting for transfers between devices, shards(): lax.all_to_all(partial_value.astype(jnp.bfloat16), 'dp', split_axis=0, co...  114 us
    all_to_all x1, blocking collectives, shards(): lax.all_to_all(outgoing, 'dp', split_axis=0, concat_axis=0, tiled=True)  96.8 us
    psum x1, waiting for transfers between devices, shards(): attended_full = lax.psum(projected.astype(jnp.bfloat16), 'expert')  71.8 us
    unnamed x3, waiting for transfers between devices  42.1 us
    gather x1, local copies, waits for them, and re-layouts, shards(): routed[token_of_slot]  17.9 us
    gather x1, local copies, waits for them, and re-layouts, shards(): returned.reshape(total_slots, model_width)[slot_of_token]  14.7 us
    unnamed x27, local copies, waits for them, and re-layouts  12.9 us
  transfers between devices with their start and end apart: 3, of which 3 were waited for; matrix products, arithmetic and copies ran while one was open for 2% of the time, Pallas kernels for 0%

commit v1 on v0

v1 whole, which is shorter than its diff:
```python
import functools
import math

import jax
import jax.numpy as jnp
from jax import lax
from jax.experimental import pallas as pl
from jax.experimental.pallas import tpu as pltpu
from jax.sharding import Mesh, PartitionSpec as P

HD = 128
EPSILON = 1e-05
BF16 = jnp.bfloat16
F32 = jnp.float32
ANY = pl.BlockSpec(memory_space=pl.ANY)
VMEM = pl.BlockSpec(memory_space=pltpu.VMEM)


def params(mib=20):
    return pltpu.CompilerParams(vmem_limit_bytes=mib * 1024 * 1024)


HOPS = (2, 1, -1, 0)
TOKEN = jax.ShapeDtypeStruct((8, 128), F32)


def chip_at(hop):
    return lax.rem(lax.axis_index("x") + hop + 4, 4)


def column_copies(w_ref, targets, others, sems):
    core = lax.axis_index("c")
    width = targets[0].shape[1]
    copies = []
    for k, (hop, target) in enumerate(zip(HOPS, targets)):
        start = pl.multiple_of((2 * chip_at(hop) + (1 - core if others else core)) * width, 128)
        copy = pltpu.make_async_copy(w_ref.at[:, pl.ds(start, width)], target, sems.at[k])
        copy.start()
        copies.append(copy)
    return copies


def column_shape(w, width, n):
    return jax.ShapeDtypeStruct((n, w.shape[0], width), BF16)


def columns_kernel(w_ref, own_ref, far_ref, rest_ref, token_ref, sems, other_sems):
    token_ref[...] = jnp.zeros_like(token_ref)
    count = len(HOPS)
    others = [far_ref.at[0]] + [rest_ref.at[k] for k in range(count - 1)]
    copies = column_copies(w_ref, others, True, other_sems)
    copies += column_copies(w_ref, [own_ref.at[k] for k in range(count)], False, sems)
    for copy in copies:
        copy.wait()


def columns(w, width):
    count = len(HOPS)
    return pl.pallas_call(
        columns_kernel,
        in_specs=[ANY],
        out_specs=[VMEM] * 4,
        out_shape=[column_shape(w, width, n) for n in (count, 1, count - 1)] + [TOKEN],
        scratch_shapes=[pltpu.SemaphoreType.DMA((count,)), pltpu.SemaphoreType.DMA((count,))],
        compiler_params=params(52),
        name="columns",
    )(w)


def attend_kernel(halves, lengths_ref, q_ref, k_ref, v_ref, after_ref, out_ref):
    seq_len, head_width = q_ref.shape
    rows = seq_len // halves
    sequence = lax.axis_index("dp")
    for part in range(halves):
        first = part * rows
        span = first + rows
        row_at = lax.broadcasted_iota(jnp.int32, (rows, 1), 0) + first
        col_at = lax.broadcasted_iota(jnp.int32, (1, span), 1)
        bound = jnp.int32(0)
        row_doc = jnp.zeros((rows, 1), jnp.int32)
        col_doc = jnp.zeros((1, span), jnp.int32)
        for i in range(lengths_ref.shape[0]):
            bound = bound + lengths_ref[i, sequence]
            row_doc = row_doc + (row_at >= bound).astype(jnp.int32)
            col_doc = col_doc + (col_at >= bound).astype(jnp.int32)
        allowed = (row_doc == col_doc) & (col_at <= row_at)
        keys = k_ref[:span, :]
        values = v_ref[:span, :]
        for h in range(head_width // HD):
            cols = slice(h * HD, (h + 1) * HD)
            scores = lax.dot_general(
                q_ref[first:span, cols],
                keys,
                (((1,), (1,)), ((), ())),
                preferred_element_type=F32,
            ) * (1.0 / math.sqrt(HD))
            scores = jnp.where(allowed, scores, -1e30)
            raised = jnp.exp(scores - jnp.max(scores, axis=1, keepdims=True))
            share = 1.0 / jnp.sum(raised, axis=1, keepdims=True)
            mixed = jnp.dot((raised * share).astype(BF16), values, preferred_element_type=F32)
            out_ref[first:span, cols] = mixed.astype(BF16)


def attend(lengths, queries, keys, values, after):
    return pl.pallas_call(
        functools.partial(attend_kernel, 2),
        out_shape=jax.ShapeDtypeStruct(queries.shape, BF16),
        in_specs=[pl.BlockSpec(memory_space=pltpu.SMEM), VMEM, VMEM, VMEM, ANY],
        out_specs=VMEM,
        compiler_params=params(),
        name="attend",
    )(lengths.T, queries, keys, values, after)


def weights_kernel(count, hops, down_ref, gate_ref, up_ref, *refs):
    own_ref, other_ref, g_ref, u_ref, token_ref, sems, other_sems, row_sems = refs[count:]
    token_ref[...] = jnp.zeros_like(token_ref)
    copies = []
    for target, others, used in ((other_ref, True, other_sems), (own_ref, False, sems)):
        copies += column_copies(down_ref, [target.at[k] for k in range(len(HOPS))], others, used)
    core = lax.axis_index("c")
    width = own_ref.shape[2]
    for k, hop in enumerate(hops):
        for j, place in enumerate((core, 1 - core)):
            start = pl.multiple_of((2 * chip_at(hop) + place) * width, 128)
            target = pl.ds((2 * k + j) * width, width)
            for i, (source, buffer) in enumerate(((gate_ref, g_ref), (up_ref, u_ref))):
                copy = pltpu.make_async_copy(
                    source.at[pl.ds(start, width), :], buffer.at[target, :], row_sems.at[4 * k + 2 * j + i]
                )
                copy.start()
                copies.append(copy)
    for copy in copies:
        copy.wait()


def expert_weights(down, gate, up, width, hops, after):
    rows = jax.ShapeDtypeStruct(gate.shape, BF16)
    return pl.pallas_call(
        functools.partial(weights_kernel, len(after), hops),
        in_specs=[ANY] * 3 + [ANY] * len(after),
        out_specs=[VMEM] * 5,
        out_shape=[column_shape(down, width, len(HOPS))] * 2 + [rows, rows, TOKEN],
        scratch_shapes=[
            pltpu.SemaphoreType.DMA((len(HOPS),)),
            pltpu.SemaphoreType.DMA((len(HOPS),)),
            pltpu.SemaphoreType.DMA((4 * len(hops),)),
        ],
        compiler_params=params(43),
        name="expert_weights",
    )(down, gate, up, *after)


def far_kernel(x_ref, xs_ref, w_ref, ws_ref, up_ref, low_ref):
    half = up_ref.shape[0]
    value = jnp.dot(x_ref[...], w_ref[0], preferred_element_type=F32)
    value = value + jnp.dot(xs_ref[...], ws_ref[0], preferred_element_type=F32)
    up_ref[...] = value[:half].astype(BF16)
    low_ref[...] = value[half:].astype(BF16)


def near_kernel(shared, x_ref, xs_ref, w_ref, ws_ref, after_ref, near_low, near_up, next_up, next_low, own_ref):
    half = near_up.shape[0]
    x, xs = x_ref[...], xs_ref[...]

    def product(k):
        value = jnp.dot(x, w_ref[k], preferred_element_type=F32)
        return value + jnp.dot(xs, ws_ref[k if shared else k - 1], preferred_element_type=F32)

    value = product(1)
    next_up[...] = value[:half]
    near_low[...] = value[half:].astype(BF16)
    value = product(2)
    near_up[...] = value[:half].astype(BF16)
    next_low[...] = value[half:]
    own_ref[...] = product(3)


def next_kernel(next_up, next_low, far_up, far_low, up_ref, low_ref):
    up_ref[...] = (next_up[...] + far_up[...].astype(F32)).astype(BF16)
    low_ref[...] = (next_low[...] + far_low[...].astype(F32)).astype(BF16)


def own_kernel(attention, count, own_ref, *refs):
    arrived = refs[:4]
    half = arrived[0].shape[0]
    for lower in range(2):
        rows = slice(lower * half, (lower + 1) * half)
        value = own_ref[rows, :]
        for ref in arrived[2 * lower : 2 * lower + 2]:
            value = value + ref[...].astype(F32)
        if attention:
            residual_ref, slot_ref = refs[4:6]
            out_ref, slots_ref = refs[6 + count :]
            value = value + residual_ref[rows, :].astype(F32)
        else:
            out_ref = refs[4 + count]
        out_ref[rows, :] = value.astype(BF16)
    if attention:
        places = lax.broadcasted_iota(jnp.int32, (slots_ref.shape[0], 1), 0)
        pick = (places == slot_ref[...]).astype(F32).astype(BF16)
        slots_ref[...] = jnp.dot(pick, out_ref[...], preferred_element_type=F32).astype(BF16)


def call(kernel, inputs, outs, name, after=(), flops=0):
    return pl.pallas_call(
        kernel,
        in_specs=[VMEM] * len(inputs) + [ANY] * len(after),
        out_specs=[VMEM] * len(outs),
        out_shape=[jax.ShapeDtypeStruct(shape, dtype) for shape, dtype in outs],
        cost_estimate=pl.CostEstimate(flops=flops, bytes_accessed=1024, transcendentals=0),
        compiler_params=params(),
        name=name,
    )(*inputs, *after)


def swap(x):
    return lax.ppermute(x, "c", [(0, 1), (1, 0)])


def shift(x, by):
    size = lax.axis_size("x")
    return lax.ppermute(x, "x", [(i, (i + by) % size) for i in range(size)])


def reduce_blocks(x, w, far_w, rest_w, attention=(), slots=None, middle=None):
    xs = swap(x)
    rows, depth = x.shape
    width = far_w.shape[2]
    half = ((rows // 2, width), BF16)
    half_f32 = ((rows // 2, width), F32)
    flops = 4 * rows * depth * width
    far = call(far_kernel, (x, xs, w, far_w), [half] * 2, "far_blocks", flops=flops)
    far_up, far_low = shift(far[0], 1), shift(far[1], -1)
    near_low, near_up, next_up, next_low, own = call(
        functools.partial(near_kernel, rest_w is far_w),
        (x, xs, w, rest_w, far[0]),
        [half, half, half_f32, half_f32, ((rows, width), F32)],
        "near_blocks",
        flops=3 * flops,
    )
    near_low, near_up = shift(near_low, 1), shift(near_up, -1)
    last = call(next_kernel, (next_up, next_low, far_up, far_low), [half] * 2, "next_blocks")
    last_up, last_low = shift(last[0], 1), shift(last[1], -1)
    inputs = [own, near_up, last_up, near_low, last_low]
    outs = [((rows, width), BF16)]
    if attention:
        inputs += attention
        outs.append(((slots, width), BF16))
    between = middle(last[0]) if middle else ()
    kernel = functools.partial(own_kernel, bool(attention), len(between[-1:]))
    return call(kernel, inputs, outs, "own_block", between[-1:]), between


def hidden_kernel(begin, end, offset, features, count, *refs):
    x_refs = refs[:count]
    wg_ref, wu_ref, wr_ref = refs[count : count + 3]
    rest = refs[count + 3 :]
    width = x_refs[0].shape[1]
    x = jnp.concatenate([ref[...] for ref in x_refs], axis=1)
    span = slice(offset * width, (offset + count) * width)
    wide = x.astype(F32)
    squares = jnp.sum(wide * wide, axis=1, keepdims=True)
    logits = jnp.sum(wide * wr_ref[:, span], axis=1, keepdims=True)
    gate = jnp.dot(x, wg_ref[span, :], preferred_element_type=F32)
    up = jnp.dot(x, wu_ref[span, :], preferred_element_type=F32)
    if not begin:
        gate, up = rest[0][...] + gate, rest[1][...] + up
        squares, logits = rest[2][...] + squares, rest[3][...] + logits
        rest = rest[4:]
    if not end:
        for ref, value in zip(rest, (gate, up, squares, logits)):
            ref[...] = value
        return
    inverse = lax.rsqrt(squares / features + EPSILON)
    scale = inverse / (1.0 + jnp.exp(-logits * inverse))
    gate = gate * scale
    rest[0][...] = (gate / (1.0 + jnp.exp(-gate)) * (up * scale)).astype(BF16)


def hidden_units(shards, offset, weights, begun=(), end=True):
    rows, width = shards[0].shape
    features, units = weights[0].shape
    outs = [((rows, units), BF16)] if end else [((rows, n), F32) for n in (units, units, 1, 1)]
    kernel = functools.partial(hidden_kernel, not begun, end, offset, features, len(shards))
    flops = 4 * rows * units * width * len(shards)
    return call(kernel, (*shards, *weights, *begun), outs, "hidden", flops=flops)


def halves_kernel(behind_ref, ahead_ref, *refs):
    up_ref, low_ref = refs[-2:]
    half = up_ref.shape[0]
    up_ref[...] = behind_ref[:half, :]
    low_ref[...] = ahead_ref[half:, :]


def join_kernel(up_ref, low_ref, *refs):
    half = up_ref.shape[0]
    refs[-1][:half, :] = up_ref[...]
    refs[-1][half:, :] = low_ref[...]


def from_slots_kernel(slot_ref, x_ref, out_ref):
    places = lax.broadcasted_iota(jnp.int32, (1, x_ref.shape[0]), 1)
    pick = (slot_ref[...] == places).astype(F32).astype(BF16)
    out_ref[...] = jnp.dot(pick, x_ref[...], preferred_element_type=F32).astype(BF16)


def shards(
    residual, queries, keys, values, lengths, w_out, w_router, expert_ids, w_gate, w_up, w_down
):
    seq_len = queries.shape[0]
    width = residual.shape[1]
    dp_count = lax.axis_size("dp")
    x_count = lax.axis_size("x")
    expert_count = w_router.shape[1]
    capacity = 3 * seq_len // (2 * expert_count)
    slots = expert_count * capacity

    same = expert_ids[:, None] == expert_ids[None, :]
    token_at = jnp.arange(seq_len, dtype=jnp.int32)
    rank = jnp.sum((same & (token_at[None, :] < token_at[:, None])).astype(jnp.int32), axis=1)
    slot = expert_ids * capacity + rank

    arrival = (0, -1, 1, 2)
    core = lax.axis_index("c")
    router = lax.dynamic_index_in_dim(w_router.astype(F32).T, lax.axis_index("dp"), 0, keepdims=False)
    router = router.reshape(x_count, 2, width)
    router = jnp.where(core == 0, router, router[:, ::-1])
    chips = (lax.axis_index("x") + jnp.array(arrival) + x_count) % x_count
    router = router[chips].reshape(1, -1)

    w_own, w_far, w_rest, token = columns(w_out, width)
    context = attend(lengths, queries, keys, values, token)

    def meanwhile(done):
        return expert_weights(w_down[0], w_gate[0], w_up[0], width, arrival, (done, router))

    (attended, outgoing), ready = reduce_blocks(
        context, w_own, swap(w_far), swap(w_rest), [residual, slot.reshape(1, -1)], slots, meanwhile
    )
    down_own, down_other, gate, up, _ = ready
    down_other = swap(down_other)

    def exchange(x):
        x = x.reshape(dp_count, slots // dp_count, width)
        return lax.all_to_all(x, "dp", split_axis=0, concat_axis=0, tiled=True).reshape(slots, width)

    here = exchange(outgoing)
    weights = (gate, up, router)
    behind, ahead = shift(here, 1), shift(here, -1)
    half = ((slots // 2, width), BF16)
    behind_up, ahead_low = call(halves_kernel, (behind, ahead), [half] * 2, "halves")
    far_up, far_low = shift(behind_up, 1), shift(ahead_low, -1)
    near = [here, swap(here), behind, swap(behind), ahead, swap(ahead)]
    begun = hidden_units(near, 0, weights, end=False)
    (far,) = call(
        join_kernel, (far_up, far_low), [((slots, width), BF16)], "join", after=(begun[2],)
    )
    (hidden,) = hidden_units([far, swap(far)], 6, weights, begun)
    (summed,), _ = reduce_blocks(hidden, down_own, down_other, down_other)
    (expert_out,) = call(
        lambda s, x, o: from_slots_kernel(s, x, o),
        (slot.reshape(-1, 1), exchange(summed)),
        [((seq_len, width), BF16)],
        "from_slots",
    )
    return (attended, expert_out)


def solution(mesh):
    chips = mesh.shape["expert"] // 2
    fine = Mesh(mesh.devices.reshape(mesh.shape["dp"], chips, 2), ("dp", "x", "c"))
    e = ("x", "c")
    in_specs = (
        P("dp", e),
        P("dp", e),
        P("dp", e),
        P("dp", e),
        P(),
        P(e, None),
        P(),
        P("dp"),
        P("dp", None, e),
        P("dp", None, e),
        P("dp", e, None),
    )
    out_specs = (P("dp", e), P("dp", e))
    return jax.shard_map(shards, mesh=fine, in_specs=in_specs, out_specs=out_specs, check_vma=False)
```

time: 453 us -> 185 us (0.41)
  waiting for transfers between devices: 228 us -> 71.2 us
  blocking collectives: 96.8 us -> 23.8 us
  Pallas kernels: 0 us -> 46.8 us
  local copies, waits for them, and re-layouts: 52.9 us -> 11 us
  matrix products: 29.3 us -> 0 us
  other arithmetic: 25.7 us -> 1.23 us
  starting transfers between devices: 5.04 us -> 29.1 us
  between operations: 14.3 us -> 0.93 us
    all_to_all x1, waiting for transfers between devices: 114 us -> 16.4 us  [exchange(): lax.all_to_all(x, 'dp', split_axis=0, concat_axis=0, tiled=True)]
    all_to_all x1, blocking collectives: 96.8 us -> 23.8 us  [exchange(): lax.all_to_all(x, 'dp', split_axis=0, concat_axis=0, tiled=True)]
    psum x1 -> x0, waiting for transfers between devices: 71.8 us -> none  [shards(): attended_full = lax.psum(projected.astype(jnp.bfloat16), 'expert')]
    ppermute x0 -> x25, waiting for transfers between devices: none -> 54.8 us  [the longest x16 50 us: shift(): return lax.ppermute(x, 'x', [(i, (i + by) % size) for i in range(size)])]
    pallas_call x0 -> x16, Pallas kernels: none -> 46.8 us  [the longest x13 29 us: call(): pl.pallas_call(kernel, in_specs=[VMEM] * len(inputs) + [ANY] * len(after)...]
    unnamed x3 -> x0, waiting for transfers between devices: 42.1 us -> none
    gather x2 -> x1, local copies, waits for them, and re-layouts: 32.6 us -> 0.58 us  [shards(): router = router[chips].reshape(1, -1)]
    dot_general x7 -> x0, matrix products: 29.3 us -> none  [the longest x1 6.81 us: shards(): projected = jnp.dot(context, w_out, preferred_element_type=jnp.float32)]
  transfers between devices with their start and end apart: 3 -> 26, of which waited for: 3 -> 14; matrix products, arithmetic and copies ran while one was open for 2% -> 1% of each run, Pallas kernels for 0% -> 19%
where the time goes in v1:
time: 185 us; the launch traced here: 184 us
  waiting for transfers between devices  71.2 us (38%)
  Pallas kernels  46.8 us (25%)
  starting transfers between devices  29.1 us (16%)
  blocking collectives  23.8 us (13%)
  local copies, waits for them, and re-layouts  11 us (6%)
    ppermute x16, waiting for transfers between devices, shift(): return lax.ppermute(x, 'x', [(i, (i + by) % size) for i in range(size)])  50 us
    pallas_call x13, Pallas kernels, call(): pl.pallas_call(kernel, in_specs=[VMEM] * len(inputs) + [ANY] * len(after)...  29 us
    ppermute x16, starting transfers between devices, shift(): return lax.ppermute(x, 'x', [(i, (i + by) % size) for i in range(size)])  23.9 us
    all_to_all x1, blocking collectives, exchange(): lax.all_to_all(x, 'dp', split_axis=0, concat_axis=0, tiled=True)  23.8 us
    all_to_all x1, waiting for transfers between devices, exchange(): lax.all_to_all(x, 'dp', split_axis=0, concat_axis=0, tiled=True)  16.4 us
    unnamed x36, local copies, waits for them, and re-layouts  10.1 us
    pallas_call x1, Pallas kernels, expert_weights(): pl.pallas_call(functools.partial(weights_kernel, len(after), hops), in_sp...  8.13 us
    pallas_call x1, Pallas kernels, columns(): pl.pallas_call(columns_kernel, in_specs=[ANY], out_specs=[VMEM] * 4, out_...  5.56 us
  transfers between devices with their start and end apart: 26, of which 14 were waited for; matrix products, arithmetic and copies ran while one was open for 1% of the time, Pallas kernels for 19%

profile of v1, /device:TPU:0, one launch (start us, length us, event | category | flops | bytes accessed | tf_op | source)
XLA Modules:
  0.0 184.2 jit_solution(8337255766166564391)
XLA Ops:
  0.7 5.6 %columns.1 = (bf16[4,640,640]{2,1,0:T(8,128)(2,1)}, bf16[1,640,640]{2,1,0:T(8,128)(2,1)S(1)}, bf16[3,640,640]{2,1,0:T(8,128)(2,1)}, f32[8,128]{1,0:T(8,128)S(1)}) custom-call(bf16[640,5120]{1,0:T(8,128)(2,1)} %w_ref.1), custom_call_target="tpu_custom_call" | custom-call | tf_op jit(solution)/shard_map/columns/pallas_call | solution.py:59
  6.9 4.1 %attend.1.x_ref = bf16[512,640]{1,0:T(8,128)(2,1)S(1)} custom-call(s32[8,16]{1,0:T(8,128)S(1)} %bitcast.21, bf16[512,640]{1,0:T(8,128)(2,1)S(1)} %copy-done.8, bf16[512,128]{1,0:T(8,128)(2,1)S(1)} %copy-done.13, bf16[512,128]{1,0:T(8,128)(2,1)S(1)} %copy-done.14, f32[8,128]{1,0:T(8,128)S(1)} %get-tuple-element.37.after_ref), custom_call_target="tpu_custom_call" | custom-call | tf_op jit(solution)/shard_map/attend/pallas_call | solution.py:105
  11.1 0.8 copy-done.3
  12.0 1.0 fusion.1
  13.2 0.8 copy-done.10
  14.1 0.9 copy-done.6
  15.0 1.9 %copy-done.1 = bf16[4,640,640]{2,1,0:T(8,128)(2,1)S(1)} copy-done((bf16[4,640,640]{2,1,0:T(8,128)(2,1)S(1)}, bf16[4,640,640]{2,1,0:T(8,128)(2,1)}, u32[]{:S(2)}) %copy-start.1) | copy-done | bytes 3276824
  16.9 1.1 copy-done.4
  18.0 1.1 copy-done.7
  19.2 1.1 copy-done.11
  20.3 2.2 %far_blocks.2 = (bf16[256,640]{1,0:T(8,128)(2,1)}, bf16[256,640]{1,0:T(8,128)(2,1)}) custom-call(bf16[512,640]{1,0:T(8,128)(2,1)S(1)} %copy-done.4, bf16[512,640]{1,0:T(8,128)(2,1)S(1)} %copy-done.11, bf16[4,640,640]{2,1,0:T(8,128)(2,1)S(1)} %copy-done.1, bf16[1,640,640]{2,1,0:T(8,128)(2,1)S(1)} %copy-done.7), custom_call_target="tpu_custom_call" | custom-call | flops 838860800 | bytes 1024 | tf_op jit(solution)/shard_map/far_blocks/pallas_call | solution.py:206
  22.4 1.6 collective-permute-start.4
  24.0 1.7 collective-permute-start.5
  25.7 0.6 gather_fusion
  26.3 1.1 copy-done.5
  27.4 1.1 copy-done.12
  28.5 5.4 %near_blocks.2 = (bf16[256,640]{1,0:T(8,128)(2,1)S(1)}, bf16[256,640]{1,0:T(8,128)(2,1)S(1)}, f32[256,640]{1,0:T(8,128)S(1)}, f32[256,640]{1,0:T(8,128)S(1)}, f32[512,640]{1,0:T(8,128)S(1)}) custom-call(bf16[512,640]{1,0:T(8,128)(2,1)S(1)} %copy-done.5, bf16[512,640]{1,0:T(8,128)(2,1)S(1)} %copy-done.12, bf16[4,640,640]{2,1,0:T(8,128)(2,1)S(1)} %copy-done.2, ...), custom_call_target="tpu_custom_call" | custom-call | flops 2516582400 | bytes 1024 | tf_op jit(solution)/shard_map/near_blocks/pallas_call | solution.py:206
  34.1 1.2 next_blocks.2
  35.3 1.6 collective-permute-start.6
  36.9 1.7 collective-permute-start.8
  38.6 1.7 collective-permute-start.3
  40.9 8.1 %expert_weights.1 = (bf16[4,512,640]{2,1,0:T(8,128)(2,1)S(1)}, bf16[4,512,640]{2,1,0:T(8,128)(2,1)S(1)}, bf16[5120,512]{1,0:T(8,128)(2,1)S(1)}, bf16[5120,512]{1,0:T(8,128)(2,1)}, f32[8,128]{1,0:T(8,128)S(1)}) custom-call(bf16[512,5120]{1,0:T(8,128)(2,1)} %bitcast.22, bf16[5120,512]{1,0:T(8,128)(2,1)} %bitcast.23, bf16[5120,512]{1,0:T(8,128)(2,1)} %bitcast.24, ...), custom_call_target="tpu_custom_call" | custom-call | tf_op jit(solution)/shard_map/expert_weights/pallas_call | solution.py:139
  49.1 3.5 %collective-permute-done.3.refs_0_ = bf16[256,640]{1,0:T(8,128)(2,1)S(1)} collective-permute-done((bf16[256,640]{1,0:T(8,128)(2,1)S(1)}, bf16[256,640]{1,0:T(8,128)(2,1)S(1)}, u32[]{:S(2)}, u32[]{:S(2)}) %collective-permute-start.3) | collective-permute-done | bytes 327712 | tf_op jit(solution)/shard_map/ppermute | solution.py:223
  52.9 1.4 own_block.2
  54.3 23.8 %all_to_all.10 = bf16[16,48,640]{2,1,0:T(8,128)(2,1)S(1)} all-to-all(bf16[16,48,640]{2,1,0:T(8,128)(2,1)S(1)} %bitcast.18), channel_id=1, replica_groups=mesh['dp'=16,'x'=4,'c'=2] {'dp'}, dimensions={0} | all-to-all | bytes 1966080 | tf_op jit(solution)/shard_map/all_to_all | solution.py:347
  78.1 3.2 %collective-permute-start.10 = (bf16[768,640]{1,0:T(8,128)(2,1)S(1)}, bf16[768,640]{1,0:T(8,128)(2,1)S(1)}, u32[]{:S(2)}, u32[]{:S(2)}) collective-permute-start(bf16[768,640]{1,0:T(8,128)(2,1)S(1)} %bitcast.15), channel_id=1, source_target_pairs={{0,6},{2,0},{4,2},{6,4},{1,7},{3,1},{5,3},{7,5},{8,14},{10,8},{12,... | collective-permute-start | bytes 2949128 | tf_op jit(solution)/shard_map/ppermute | solution.py:223
  81.4 19.4 %collective-permute-done.9.behind_ref.refs_2_ = bf16[768,640]{1,0:T(8,128)(2,1)S(1)} collective-permute-done((bf16[768,640]{1,0:T(8,128)(2,1)S(1)}, bf16[768,640]{1,0:T(8,128)(2,1)S(1)}, u32[]{:S(2)}, u32[]{:S(2)}) %collective-permute-start.9) | collective-permute-done | bytes 983072 | tf_op jit(solution)/shard_map/ppermute | solution.py:223
  100.7 0.5 collective-permute-start.15
  101.7 3.0 %collective-permute-start.12 = (bf16[384,640]{1,0:T(8,128)(2,1)S(1)}, bf16[384,640]{1,0:T(8,128)(2,1)S(1)}, u32[]{:S(2)}, u32[]{:S(2)}) collective-permute-start(bf16[384,640]{1,0:T(8,128)(2,1)S(1)} %get-tuple-element.54), channel_id=1, source_target_pairs={{0,6},{2,0},{4,2},{6,4},{1,7},{3,1},{5,3},{7,5},{8,14},{10,8},{12,... | collective-permute-start | bytes 1474568 | tf_op jit(solution)/shard_map/ppermute | solution.py:223
  104.7 7.7 %hidden.2 = (f32[768,512]{1,0:T(8,128)S(1)}, f32[768,512]{1,0:T(8,128)S(1)}, f32[768,1]{1,0:T(8,128)S(1)}, f32[768,1]{1,0:T(8,128)S(1)}) custom-call(bf16[768,640]{1,0:T(8,128)(2,1)S(1)} %bitcast.17, bf16[768,640]{1,0:T(8,128)(2,1)S(1)} %collective-permute-done.13.refs_1_, bf16[768,640]{1,0:T(8,128)(2,1)S(1)} %collective-permute-done.9.behind_ref.refs_2_, ...), custom_call_target="tpu_custom_call" | custom-call | flops 6039797760 | bytes 1024 | tf_op jit(solution)/shard_map/hidden/pallas_call | solution.py:206
  112.4 3.9 %collective-permute-done.11.up_ref = bf16[384,640]{1,0:T(8,128)(2,1)S(1)} collective-permute-done((bf16[384,640]{1,0:T(8,128)(2,1)S(1)}, bf16[384,640]{1,0:T(8,128)(2,1)S(1)}, u32[]{:S(2)}, u32[]{:S(2)}) %collective-permute-start.11) | collective-permute-done | bytes 491552 | tf_op jit(solution)/shard_map/ppermute | solution.py:223
  116.4 2.6 %collective-permute-done.16.refs_1_ = bf16[768,640]{1,0:T(8,128)(2,1)S(1)} collective-permute-done((bf16[768,640]{1,0:T(8,128)(2,1)S(1)}, bf16[768,640]{1,0:T(8,128)(2,1)S(1)}, u32[]{:S(2)}, u32[]{:S(2)}) %collective-permute-start.16) | collective-permute-done | bytes 983072 | tf_op jit(solution)/shard_map/ppermute | solution.py:218
  119.0 2.6 %hidden.3.x_ref = bf16[768,512]{1,0:T(8,128)(2,1)S(1)} custom-call(bf16[768,640]{1,0:T(8,128)(2,1)S(1)} %join.1.refs_0_, bf16[768,640]{1,0:T(8,128)(2,1)S(1)} %collective-permute-done.16.refs_1_, bf16[5120,512]{1,0:T(8,128)(2,1)S(1)} %get-tuple-element.55.refs_6_.refs_2_, bf16[5120,512]{1,0:T(8,128)(2,1)S(1)} %copy-done, ...), custom_call_target="tpu_custom_call" | custom-call | flops 2013265920 | bytes 1024 | tf_op jit(solution)/shard_map/hidden/pallas_call | solution.py:206
  121.8 2.2 %collective-permute-done.17.xs_ref = bf16[768,512]{1,0:T(8,128)(2,1)S(1)} collective-permute-done((bf16[768,512]{1,0:T(8,128)(2,1)S(1)}, bf16[768,512]{1,0:T(8,128)(2,1)S(1)}, u32[]{:S(2)}, u32[]{:S(2)}) %collective-permute-start.17) | collective-permute-done | bytes 786464 | tf_op jit(solution)/shard_map/ppermute | solution.py:218
  123.9 1.4 far_blocks.3
  125.4 0.7 collective-permute-start.20
  126.1 2.6 %collective-permute-start.21 = (bf16[384,640]{1,0:T(8,128)(2,1)S(1)}, bf16[384,640]{1,0:T(8,128)(2,1)S(1)}, u32[]{:S(2)}, u32[]{:S(2)}) collective-permute-start(bf16[384,640]{1,0:T(8,128)(2,1)S(1)} %get-tuple-element.68), channel_id=1, source_target_pairs={{0,6},{2,0},{4,2},{6,4},{1,7},{3,1},{5,3},{7,5},{8,14},{10,8},{12,... | collective-permute-start | bytes 1474568 | tf_op jit(solution)/shard_map/ppermute | solution.py:223
  128.7 3.9 %near_blocks.3 = (bf16[384,640]{1,0:T(8,128)(2,1)S(1)}, bf16[384,640]{1,0:T(8,128)(2,1)S(1)}, f32[384,640]{1,0:T(8,128)S(1)}, f32[384,640]{1,0:T(8,128)S(1)}, f32[768,640]{1,0:T(8,128)S(1)}) custom-call(bf16[768,512]{1,0:T(8,128)(2,1)S(1)} %hidden.3.x_ref, bf16[768,512]{1,0:T(8,128)(2,1)S(1)} %collective-permute-done.17.xs_ref, ...), custom_call_target="tpu_custom_call" | custom-call | flops 3019898880 | bytes 1024 | tf_op jit(solution)/shard_map/near_blocks/pallas_call | solution.py:206
  132.6 1.8 collective-permute-start.19
  134.7 6.0 %collective-permute-done.20.far_up = bf16[384,640]{1,0:T(8,128)(2,1)S(1)} collective-permute-done((bf16[384,640]{1,0:T(8,128)(2,1)S(1)}, bf16[384,640]{1,0:T(8,128)(2,1)S(1)}, u32[]{:S(2)}, u32[]{:S(2)}) %collective-permute-start.20) | collective-permute-done | bytes 491552 | tf_op jit(solution)/shard_map/ppermute | solution.py:223
  140.9 1.2 collective-permute-start.22
  142.1 2.2 %collective-permute-start.24 = (bf16[384,640]{1,0:T(8,128)(2,1)S(1)}, bf16[384,640]{1,0:T(8,128)(2,1)S(1)}, u32[]{:S(2)}, u32[]{:S(2)}) collective-permute-start(bf16[384,640]{1,0:T(8,128)(2,1)S(1)} %get-tuple-element.71), channel_id=1, source_target_pairs={{0,6},{2,0},{4,2},{6,4},{1,7},{3,1},{5,3},{7,5},{8,14},{10,8},{12,... | collective-permute-start | bytes 1474568 | tf_op jit(solution)/shard_map/ppermute | solution.py:223
  144.3 6.5 %collective-permute-done.19.refs_0_ = bf16[384,640]{1,0:T(8,128)(2,1)S(1)} collective-permute-done((bf16[384,640]{1,0:T(8,128)(2,1)S(1)}, bf16[384,640]{1,0:T(8,128)(2,1)S(1)}, u32[]{:S(2)}, u32[]{:S(2)}) %collective-permute-start.19) | collective-permute-done | bytes 491552 | tf_op jit(solution)/shard_map/ppermute | solution.py:223
  151.2 9.7 %collective-permute-done.22.refs_1_ = bf16[384,640]{1,0:T(8,128)(2,1)S(1)} collective-permute-done((bf16[384,640]{1,0:T(8,128)(2,1)S(1)}, bf16[384,640]{1,0:T(8,128)(2,1)S(1)}, u32[]{:S(2)}, u32[]{:S(2)}) %collective-permute-start.22) | collective-permute-done | bytes 491552 | tf_op jit(solution)/shard_map/ppermute | solution.py:223
  161.0 1.3 own_block.3
  162.3 3.6 %all-to-all-start.1 = ((bf16[16,48,640]{2,1,0:T(8,128)(2,1)}), bf16[16,48,640]{2,1,0:T(8,128)(2,1)S(1)}, u32[]{:S(2)}, u32[]{:S(2)}) async-start(bf16[16,48,640]{2,1,0:T(8,128)(2,1)} %bitcast.8), calls=%async_computation.1 | async-start | bytes 1966080 | tf_op jit(solution)/shard_map/all_to_all | solution.py:347
  166.1 16.4 %all-to-all-done.1 = bf16[16,48,640]{2,1,0:T(8,128)(2,1)S(1)} async-done(((bf16[16,48,640]{2,1,0:T(8,128)(2,1)}), bf16[16,48,640]{2,1,0:T(8,128)(2,1)S(1)}, u32[]{:S(2)}, u32[]{:S(2)}) %all-to-all-start.1) | async-done | bytes 983072 | tf_op jit(solution)/shard_map/all_to_all | solution.py:347
  182.5 1.7 from_slots.1
  (68 shorter events, 4.2 us)
Async XLA Ops:
  0.6 12.5 %copy-start.17 = (s32[4]{0:T(128)S(1)}, s32[4]{0:T(128)}, u32[]{:S(2)}) copy-start(s32[4]{0:T(128)} %constant.40.clone) | copy-start | bytes 52
  0.6 6.2 %copy-start.15 = (s32[16,8]{0,1:T(8,128)S(1)}, s32[16,8]{0,1:T(8,128)}, u32[]{:S(2)}) copy-start(s32[16,8]{0,1:T(8,128)} %param.16) | copy-start | bytes 1540
  0.7 6.2 %copy-start.8 = (bf16[512,640]{1,0:T(8,128)(2,1)S(1)}, bf16[512,640]{1,0:T(8,128)(2,1)}, u32[]{:S(2)}) copy-start(bf16[512,640]{1,0:T(8,128)(2,1)} %q_ref.1) | copy-start | bytes 1966084
  0.7 6.2 %copy-start.13 = (bf16[512,128]{1,0:T(8,128)(2,1)S(1)}, bf16[512,128]{1,0:T(8,128)(2,1)}, u32[]{:S(2)}) copy-start(bf16[512,128]{1,0:T(8,128)(2,1)} %k_ref.1) | copy-start | bytes 393220
  0.7 6.2 %copy-start.14 = (bf16[512,128]{1,0:T(8,128)(2,1)S(1)}, bf16[512,128]{1,0:T(8,128)(2,1)}, u32[]{:S(2)}) copy-start(bf16[512,128]{1,0:T(8,128)(2,1)} %v_ref.1) | copy-start | bytes 393220
  6.2 20.1 %collective-permute-start.1 = (bf16[3,640,640]{2,1,0:T(8,128)(2,1)}, bf16[3,640,640]{2,1,0:T(8,128)(2,1)}, u32[]{:S(2)}, u32[]{:S(2)}) collective-permute-start(bf16[3,640,640]{2,1,0:T(8,128)(2,1)} %get-tuple-element.39), channel_id=1, source_target_pairs={{0,1},{1,0},{2,3},{3,2},{4,5},{5,4},{6,7},{7,6},{8,9},{9,8},{10,11... | collective-permute-start | bytes 7372808 | tf_op jit(solution)/shard_map/ppermute | solution.py:218
  6.3 7.7 %collective-permute-start.2 = (bf16[1,640,640]{2,1,0:T(8,128)(2,1)S(1)}, bf16[1,640,640]{2,1,0:T(8,128)(2,1)S(1)}, u32[]{:S(2)}, u32[]{:S(2)}) collective-permute-start(bf16[1,640,640]{2,1,0:T(8,128)(2,1)S(1)} %get-tuple-element.40), channel_id=1, source_target_pairs={{0,1},{1,0},{2,3},{3,2},{4,5},{5,4},{6,7},{7,6},{8,9},{9,8},{10,11... | collective-permute-start | bytes 2457608 | tf_op jit(solution)/shard_map/ppermute | solution.py:218
  11.0 2.2 %collective-permute-start = (bf16[512,640]{1,0:T(8,128)(2,1)S(1)}, bf16[512,640]{1,0:T(8,128)(2,1)S(1)}, u32[]{:S(2)}, u32[]{:S(2)}) collective-permute-start(bf16[512,640]{1,0:T(8,128)(2,1)S(1)} %attend.1.x_ref), channel_id=1, source_target_pairs={{0,1},{1,0},{2,3},{3,2},{4,5},{5,4},{6,7},{7,6},{8,9},{9,8},{10,11... | collective-permute-start | bytes 1966088 | tf_op jit(solution)/shard_map/ppermute | solution.py:218
  11.1 0.8 copy-start.3
  13.2 0.8 copy-start.10
  14.1 0.9 copy-start.6
  15.0 1.9 %copy-start.1 = (bf16[4,640,640]{2,1,0:T(8,128)(2,1)S(1)}, bf16[4,640,640]{2,1,0:T(8,128)(2,1)}, u32[]{:S(2)}) copy-start(bf16[4,640,640]{2,1,0:T(8,128)(2,1)} %get-tuple-element.38.w_ref) | copy-start | bytes 9830404
  16.9 1.1 copy-start.4
  18.0 1.1 copy-start.7
  19.2 1.1 copy-start.11
  20.2 6.1 %copy-start.2 = (bf16[4,640,640]{2,1,0:T(8,128)(2,1)S(1)}, bf16[4,640,640]{2,1,0:T(8,128)(2,1)}, u32[]{:S(2)}) copy-start(bf16[4,640,640]{2,1,0:T(8,128)(2,1)} %get-tuple-element.38.w_ref) | copy-start | bytes 9830404
  22.4 11.6 %collective-permute-start.4 = (bf16[256,640]{1,0:T(8,128)(2,1)}, bf16[256,640]{1,0:T(8,128)(2,1)}, u32[]{:S(2)}, u32[]{:S(2)}) collective-permute-start(bf16[256,640]{1,0:T(8,128)(2,1)} %get-tuple-element.41.after_ref), channel_id=1, source_target_pairs={{0,2},{2,4},{4,6},{6,0},{1,3},{3,5},{5,7},{7,1},{8,10},{10,12},{12... | collective-permute-start | bytes 983048 | tf_op jit(solution)/shard_map/ppermute | solution.py:223
  24.0 10.1 %collective-permute-start.5 = (bf16[256,640]{1,0:T(8,128)(2,1)}, bf16[256,640]{1,0:T(8,128)(2,1)}, u32[]{:S(2)}, u32[]{:S(2)}) collective-permute-start(bf16[256,640]{1,0:T(8,128)(2,1)} %get-tuple-element.46), channel_id=1, source_target_pairs={{0,6},{2,0},{4,2},{6,4},{1,7},{3,1},{5,3},{7,5},{8,14},{10,8},{12,... | collective-permute-start | bytes 983048 | tf_op jit(solution)/shard_map/ppermute | solution.py:223
  26.3 1.1 copy-start.5
  27.4 1.1 copy-start.12
  28.5 12.1 %copy-start.16 = (s32[512]{0:T(512)S(1)}, s32[512]{0:T(512)}, u32[]{:S(2)}) copy-start(s32[512]{0:T(512)} %param.19) | copy-start | bytes 6148
  35.3 13.7 %collective-permute-start.6 = (bf16[256,640]{1,0:T(8,128)(2,1)S(1)}, bf16[256,640]{1,0:T(8,128)(2,1)S(1)}, u32[]{:S(2)}, u32[]{:S(2)}) collective-permute-start(bf16[256,640]{1,0:T(8,128)(2,1)S(1)} %get-tuple-element.47.refs_0_), channel_id=1, source_target_pairs={{0,2},{2,4},{4,6},{6,0},{1,3},{3,5},{5,7},{7,1},{8,10},{10,12},{12... | collective-permute-start | bytes 983048 | tf_op jit(solution)/shard_map/ppermute | solution.py:223
  36.9 12.2 %collective-permute-start.8 = (bf16[256,640]{1,0:T(8,128)(2,1)S(1)}, bf16[256,640]{1,0:T(8,128)(2,1)S(1)}, u32[]{:S(2)}, u32[]{:S(2)}) collective-permute-start(bf16[256,640]{1,0:T(8,128)(2,1)S(1)} %get-tuple-element.49), channel_id=1, source_target_pairs={{0,6},{2,0},{4,2},{6,4},{1,7},{3,1},{5,3},{7,5},{8,14},{10,8},{12,... | collective-permute-start | bytes 983048 | tf_op jit(solution)/shard_map/ppermute | solution.py:223
  38.6 13.9 %collective-permute-start.3 = (bf16[256,640]{1,0:T(8,128)(2,1)S(1)}, bf16[256,640]{1,0:T(8,128)(2,1)S(1)}, u32[]{:S(2)}, u32[]{:S(2)}) collective-permute-start(bf16[256,640]{1,0:T(8,128)(2,1)S(1)} %get-tuple-element.43), channel_id=1, source_target_pairs={{0,6},{2,0},{4,2},{6,4},{1,7},{3,1},{5,3},{7,5},{8,14},{10,8},{12,... | collective-permute-start | bytes 983048 | tf_op jit(solution)/shard_map/ppermute | solution.py:223
  40.3 12.6 %collective-permute-start.7 = (bf16[256,640]{1,0:T(8,128)(2,1)S(1)}, bf16[256,640]{1,0:T(8,128)(2,1)S(1)}, u32[]{:S(2)}, u32[]{:S(2)}) collective-permute-start(bf16[256,640]{1,0:T(8,128)(2,1)S(1)} %get-tuple-element.48), channel_id=1, source_target_pairs={{0,2},{2,4},{4,6},{6,0},{1,3},{3,5},{5,7},{7,1},{8,10},{10,12},{12... | collective-permute-start | bytes 983048 | tf_op jit(solution)/shard_map/ppermute | solution.py:223
  40.9 12.0 %copy-start.9 = (bf16[512,640]{1,0:T(8,128)(2,1)S(1)}, bf16[512,640]{1,0:T(8,128)(2,1)}, u32[]{:S(2)}) copy-start(bf16[512,640]{1,0:T(8,128)(2,1)} %refs_4_.1) | copy-start | bytes 1966084
  52.9 51.8 %copy-start = (bf16[5120,512]{1,0:T(8,128)(2,1)S(1)}, bf16[5120,512]{1,0:T(8,128)(2,1)}, u32[]{:S(2)}) copy-start(bf16[5120,512]{1,0:T(8,128)(2,1)} %get-tuple-element.56.refs_7_.refs_3_) | copy-start | bytes 15728644
  78.1 22.6 %collective-permute-start.9 = (bf16[768,640]{1,0:T(8,128)(2,1)S(1)}, bf16[768,640]{1,0:T(8,128)(2,1)S(1)}, u32[]{:S(2)}, u32[]{:S(2)}) collective-permute-start(bf16[768,640]{1,0:T(8,128)(2,1)S(1)} %bitcast.14), channel_id=1, source_target_pairs={{0,2},{2,4},{4,6},{6,0},{1,3},{3,5},{5,7},{7,1},{8,10},{10,12},{12... | collective-permute-start | bytes 2949128 | tf_op jit(solution)/shard_map/ppermute | solution.py:223
  78.1 22.6 %collective-permute-start.10 = (bf16[768,640]{1,0:T(8,128)(2,1)S(1)}, bf16[768,640]{1,0:T(8,128)(2,1)S(1)}, u32[]{:S(2)}, u32[]{:S(2)}) collective-permute-start(bf16[768,640]{1,0:T(8,128)(2,1)S(1)} %bitcast.15), channel_id=1, source_target_pairs={{0,6},{2,0},{4,2},{6,4},{1,7},{3,1},{5,3},{7,5},{8,14},{10,8},{12,... | collective-permute-start | bytes 2949128 | tf_op jit(solution)/shard_map/ppermute | solution.py:223
  81.4 20.3 %collective-permute-start.13 = (bf16[768,640]{1,0:T(8,128)(2,1)S(1)}, bf16[768,640]{1,0:T(8,128)(2,1)S(1)}, u32[]{:S(2)}, u32[]{:S(2)}) collective-permute-start(bf16[768,640]{1,0:T(8,128)(2,1)S(1)} %bitcast.16), channel_id=1, source_target_pairs={{0,1},{1,0},{2,3},{3,2},{4,5},{5,4},{6,7},{7,6},{8,9},{9,8},{10,11... | collective-permute-start | bytes 2949128 | tf_op jit(solution)/shard_map/ppermute | solution.py:218
  100.7 3.9 %collective-permute-start.14 = (bf16[768,640]{1,0:T(8,128)(2,1)S(1)}, bf16[768,640]{1,0:T(8,128)(2,1)S(1)}, u32[]{:S(2)}, u32[]{:S(2)}) collective-permute-start(bf16[768,640]{1,0:T(8,128)(2,1)S(1)} %collective-permute-done.9.behind_ref.refs_2_), channel_id=1, source_target_pairs={{0,1},{1,0},{2,3},{3,2},{4,5},{5,4},{6,7},{7,6},{8,9},{9,8},{10,11... | collective-permute-start | bytes 2949128 | tf_op jit(solution)/shard_map/ppermute | solution.py:218
  100.7 4.0 %collective-permute-start.15 = (bf16[768,640]{1,0:T(8,128)(2,1)S(1)}, bf16[768,640]{1,0:T(8,128)(2,1)S(1)}, u32[]{:S(2)}, u32[]{:S(2)}) collective-permute-start(bf16[768,640]{1,0:T(8,128)(2,1)S(1)} %collective-permute-done.10.ahead_ref.refs_4_), channel_id=1, source_target_pairs={{0,1},{1,0},{2,3},{3,2},{4,5},{5,4},{6,7},{7,6},{8,9},{9,8},{10,11... | collective-permute-start | bytes 2949128 | tf_op jit(solution)/shard_map/ppermute | solution.py:218
  101.3 20.5 %collective-permute-start.18 = (bf16[4,512,640]{2,1,0:T(8,128)(2,1)S(1)}, bf16[4,512,640]{2,1,0:T(8,128)(2,1)S(1)}, u32[]{:S(2)}, u32[]{:S(2)}) collective-permute-start(bf16[4,512,640]{2,1,0:T(8,128)(2,1)S(1)} %get-tuple-element.62), channel_id=1, source_target_pairs={{0,1},{1,0},{2,3},{3,2},{4,5},{5,4},{6,7},{7,6},{8,9},{9,8},{10,11... | collective-permute-start | bytes 7864328 | tf_op jit(solution)/shard_map/ppermute | solution.py:218
  101.3 14.9 %collective-permute-start.11 = (bf16[384,640]{1,0:T(8,128)(2,1)S(1)}, bf16[384,640]{1,0:T(8,128)(2,1)S(1)}, u32[]{:S(2)}, u32[]{:S(2)}) collective-permute-start(bf16[384,640]{1,0:T(8,128)(2,1)S(1)} %get-tuple-element.53), channel_id=1, source_target_pairs={{0,2},{2,4},{4,6},{6,0},{1,3},{3,5},{5,7},{7,1},{8,10},{10,12},{12... | collective-permute-start | bytes 1474568 | tf_op jit(solution)/shard_map/ppermute | solution.py:223
  101.7 14.6 %collective-permute-start.12 = (bf16[384,640]{1,0:T(8,128)(2,1)S(1)}, bf16[384,640]{1,0:T(8,128)(2,1)S(1)}, u32[]{:S(2)}, u32[]{:S(2)}) collective-permute-start(bf16[384,640]{1,0:T(8,128)(2,1)S(1)} %get-tuple-element.54), channel_id=1, source_target_pairs={{0,6},{2,0},{4,2},{6,4},{1,7},{3,1},{5,3},{7,5},{8,14},{10,8},{12,... | collective-permute-start | bytes 1474568 | tf_op jit(solution)/shard_map/ppermute | solution.py:223
  116.3 2.6 %collective-permute-start.16 = (bf16[768,640]{1,0:T(8,128)(2,1)S(1)}, bf16[768,640]{1,0:T(8,128)(2,1)S(1)}, u32[]{:S(2)}, u32[]{:S(2)}) collective-permute-start(bf16[768,640]{1,0:T(8,128)(2,1)S(1)} %join.1.refs_0_), channel_id=1, source_target_pairs={{0,1},{1,0},{2,3},{3,2},{4,5},{5,4},{6,7},{7,6},{8,9},{9,8},{10,11... | collective-permute-start | bytes 2949128 | tf_op jit(solution)/shard_map/ppermute | solution.py:218
  121.6 2.4 %collective-permute-start.17 = (bf16[768,512]{1,0:T(8,128)(2,1)S(1)}, bf16[768,512]{1,0:T(8,128)(2,1)S(1)}, u32[]{:S(2)}, u32[]{:S(2)}) collective-permute-start(bf16[768,512]{1,0:T(8,128)(2,1)S(1)} %hidden.3.x_ref), channel_id=1, source_target_pairs={{0,1},{1,0},{2,3},{3,2},{4,5},{5,4},{6,7},{7,6},{8,9},{9,8},{10,11... | collective-permute-start | bytes 2359304 | tf_op jit(solution)/shard_map/ppermute | solution.py:218
  125.4 15.3 %collective-permute-start.20 = (bf16[384,640]{1,0:T(8,128)(2,1)S(1)}, bf16[384,640]{1,0:T(8,128)(2,1)S(1)}, u32[]{:S(2)}, u32[]{:S(2)}) collective-permute-start(bf16[384,640]{1,0:T(8,128)(2,1)S(1)} %get-tuple-element.63.after_ref), channel_id=1, source_target_pairs={{0,2},{2,4},{4,6},{6,0},{1,3},{3,5},{5,7},{7,1},{8,10},{10,12},{12... | collective-permute-start | bytes 1474568 | tf_op jit(solution)/shard_map/ppermute | solution.py:223
  126.1 14.7 %collective-permute-start.21 = (bf16[384,640]{1,0:T(8,128)(2,1)S(1)}, bf16[384,640]{1,0:T(8,128)(2,1)S(1)}, u32[]{:S(2)}, u32[]{:S(2)}) collective-permute-start(bf16[384,640]{1,0:T(8,128)(2,1)S(1)} %get-tuple-element.68), channel_id=1, source_target_pairs={{0,6},{2,0},{4,2},{6,4},{1,7},{3,1},{5,3},{7,5},{8,14},{10,8},{12,... | collective-permute-start | bytes 1474568 | tf_op jit(solution)/shard_map/ppermute | solution.py:223
  132.6 18.2 %collective-permute-start.19 = (bf16[384,640]{1,0:T(8,128)(2,1)S(1)}, bf16[384,640]{1,0:T(8,128)(2,1)S(1)}, u32[]{:S(2)}, u32[]{:S(2)}) collective-permute-start(bf16[384,640]{1,0:T(8,128)(2,1)S(1)} %get-tuple-element.65), channel_id=1, source_target_pairs={{0,6},{2,0},{4,2},{6,4},{1,7},{3,1},{5,3},{7,5},{8,14},{10,8},{12,... | collective-permute-start | bytes 1474568 | tf_op jit(solution)/shard_map/ppermute | solution.py:223
  134.4 16.8 %collective-permute-start.23 = (bf16[384,640]{1,0:T(8,128)(2,1)S(1)}, bf16[384,640]{1,0:T(8,128)(2,1)S(1)}, u32[]{:S(2)}, u32[]{:S(2)}) collective-permute-start(bf16[384,640]{1,0:T(8,128)(2,1)S(1)} %get-tuple-element.70), channel_id=1, source_target_pairs={{0,2},{2,4},{4,6},{6,0},{1,3},{3,5},{5,7},{7,1},{8,10},{10,12},{12... | collective-permute-start | bytes 1474568 | tf_op jit(solution)/shard_map/ppermute | solution.py:223
  140.9 20.1 %collective-permute-start.22 = (bf16[384,640]{1,0:T(8,128)(2,1)S(1)}, bf16[384,640]{1,0:T(8,128)(2,1)S(1)}, u32[]{:S(2)}, u32[]{:S(2)}) collective-permute-start(bf16[384,640]{1,0:T(8,128)(2,1)S(1)} %get-tuple-element.69), channel_id=1, source_target_pairs={{0,2},{2,4},{4,6},{6,0},{1,3},{3,5},{5,7},{7,1},{8,10},{10,12},{12... | collective-permute-start | bytes 1474568 | tf_op jit(solution)/shard_map/ppermute | solution.py:223
  142.1 18.9 %collective-permute-start.24 = (bf16[384,640]{1,0:T(8,128)(2,1)S(1)}, bf16[384,640]{1,0:T(8,128)(2,1)S(1)}, u32[]{:S(2)}, u32[]{:S(2)}) collective-permute-start(bf16[384,640]{1,0:T(8,128)(2,1)S(1)} %get-tuple-element.71), channel_id=1, source_target_pairs={{0,6},{2,0},{4,2},{6,4},{1,7},{3,1},{5,3},{7,5},{8,14},{10,8},{12,... | collective-permute-start | bytes 1474568 | tf_op jit(solution)/shard_map/ppermute | solution.py:223
  162.3 20.2 %all-to-all-start.1 = ((bf16[16,48,640]{2,1,0:T(8,128)(2,1)}), bf16[16,48,640]{2,1,0:T(8,128)(2,1)S(1)}, u32[]{:S(2)}, u32[]{:S(2)}) async-start(bf16[16,48,640]{2,1,0:T(8,128)(2,1)} %bitcast.8), calls=%async_computation.1 | async-start | bytes 1966080 | tf_op jit(solution)/shard_map/all_to_all | solution.py:347

commit v2 on v1

v2 whole, which is shorter than its diff:
```python
import functools
import math

import jax
import jax.numpy as jnp
from jax import lax
from jax.experimental import pallas as pl
from jax.experimental.pallas import tpu as pltpu
from jax.sharding import Mesh, PartitionSpec as P

HD = 128
EPSILON = 1e-05
BF16 = jnp.bfloat16
F32 = jnp.float32
ANY = pl.BlockSpec(memory_space=pl.ANY)
VMEM = pl.BlockSpec(memory_space=pltpu.VMEM)


def params(mib=20):
    return pltpu.CompilerParams(vmem_limit_bytes=mib * 1024 * 1024)


HOPS = (2, 1, -1, 0)
COST = pl.CostEstimate(flops=1024, bytes_accessed=1024, transcendentals=0)
TOKEN = jax.ShapeDtypeStruct((8, 128), F32)


def chip_at(hop):
    return lax.rem(lax.axis_index("x") + hop + 4, 4)


def column_copies(w_ref, targets, others, sems):
    core = lax.axis_index("c")
    width = targets[0].shape[1]
    copies = []
    for k, (hop, target) in enumerate(zip(HOPS, targets)):
        start = pl.multiple_of((2 * chip_at(hop) + (1 - core if others else core)) * width, 128)
        copy = pltpu.make_async_copy(w_ref.at[:, pl.ds(start, width)], target, sems.at[k])
        copy.start()
        copies.append(copy)
    return copies


def column_shape(w, width, n):
    return jax.ShapeDtypeStruct((n, w.shape[0], width), BF16)


def columns_kernel(w_ref, *refs):
    own_far_ref, own_rest_ref, far_ref, rest_ref, token_ref, sems, other_sems = refs[-7:]
    token_ref[...] = jnp.zeros_like(token_ref)
    copies = []
    for others, first, rest, used in ((True, far_ref, rest_ref, other_sems), (False, own_far_ref, own_rest_ref, sems)):
        targets = [first.at[0]] + [rest.at[k] for k in range(len(HOPS) - 1)]
        copies += column_copies(w_ref, targets, others, used)
    for copy in copies:
        copy.wait()


def columns(w, width, after=()):
    count = len(HOPS)
    return pl.pallas_call(
        columns_kernel,
        in_specs=[ANY] * (1 + len(after)),
        out_specs=[VMEM] * 5,
        out_shape=[column_shape(w, width, n) for n in (1, count - 1, 1, count - 1)] + [TOKEN],
        scratch_shapes=[pltpu.SemaphoreType.DMA((count,)), pltpu.SemaphoreType.DMA((count,))],
        cost_estimate=COST,
        compiler_params=params(),
        name="columns",
    )(w, *after)


def attend_kernel(halves, lengths_ref, q_ref, k_ref, v_ref, after_ref, out_ref):
    seq_len, head_width = q_ref.shape
    rows = seq_len // halves
    sequence = lax.axis_index("dp")
    for part in range(halves):
        first = part * rows
        span = first + rows
        row_at = lax.broadcasted_iota(jnp.int32, (rows, 1), 0) + first
        col_at = lax.broadcasted_iota(jnp.int32, (1, span), 1)
        bound = jnp.int32(0)
        row_doc = jnp.zeros((rows, 1), jnp.int32)
        col_doc = jnp.zeros((1, span), jnp.int32)
        for i in range(lengths_ref.shape[0]):
            bound = bound + lengths_ref[i, sequence]
            row_doc = row_doc + (row_at >= bound).astype(jnp.int32)
            col_doc = col_doc + (col_at >= bound).astype(jnp.int32)
        allowed = (row_doc == col_doc) & (col_at <= row_at)
        keys = k_ref[:span, :]
        values = v_ref[:span, :]
        for h in range(head_width // HD):
            cols = slice(h * HD, (h + 1) * HD)
            scores = lax.dot_general(
                q_ref[first:span, cols],
                keys,
                (((1,), (1,)), ((), ())),
                preferred_element_type=F32,
            ) * (1.0 / math.sqrt(HD))
            scores = jnp.where(allowed, scores, -1e30)
            raised = jnp.exp(scores - jnp.max(scores, axis=1, keepdims=True))
            share = 1.0 / jnp.sum(raised, axis=1, keepdims=True)
            mixed = jnp.dot((raised * share).astype(BF16), values, preferred_element_type=F32)
            out_ref[first:span, cols] = mixed.astype(BF16)


def attend(lengths, queries, keys, values, after):
    return pl.pallas_call(
        functools.partial(attend_kernel, 2),
        out_shape=jax.ShapeDtypeStruct(queries.shape, BF16),
        in_specs=[pl.BlockSpec(memory_space=pltpu.SMEM), VMEM, VMEM, VMEM, VMEM],
        out_specs=VMEM,
        cost_estimate=COST,
        compiler_params=params(),
        name="attend",
    )(lengths.T, queries, keys, values, after)


def far_kernel(x_ref, xs_ref, w_ref, ws_ref, up_ref, low_ref):
    half = up_ref.shape[0]
    value = jnp.dot(x_ref[...], w_ref[0], preferred_element_type=F32)
    value = value + jnp.dot(xs_ref[...], ws_ref[0], preferred_element_type=F32)
    up_ref[...] = value[:half].astype(BF16)
    low_ref[...] = value[half:].astype(BF16)


def near_kernel(x_ref, xs_ref, w_ref, ws_ref, after_ref, near_low, near_up):
    half = near_up.shape[0]
    for k, rows, out_ref in ((1, slice(half, 2 * half), near_low), (2, slice(0, half), near_up)):
        value = jnp.dot(x_ref[rows, :], w_ref[k - 1], preferred_element_type=F32)
        value = value + jnp.dot(xs_ref[rows, :], ws_ref[k - 1], preferred_element_type=F32)
        out_ref[...] = value.astype(BF16)


def rest_kernel(x_ref, xs_ref, w_ref, ws_ref, after_ref, next_up, next_low, own_ref):
    half = next_up.shape[0]
    for k, rows, out_ref in (
        (1, slice(0, half), next_up),
        (2, slice(half, 2 * half), next_low),
        (3, slice(0, 2 * half), own_ref),
    ):
        value = jnp.dot(x_ref[rows, :], w_ref[k - 1], preferred_element_type=F32)
        out_ref[...] = value + jnp.dot(xs_ref[rows, :], ws_ref[k - 1], preferred_element_type=F32)


def next_kernel(next_up, next_low, far_up, far_low, up_ref, low_ref):
    up_ref[...] = (next_up[...] + far_up[...].astype(F32)).astype(BF16)
    low_ref[...] = (next_low[...] + far_low[...].astype(F32)).astype(BF16)


def own_kernel(attention, count, own_ref, *refs):
    arrived = refs[:4]
    half = arrived[0].shape[0]
    for lower in range(2):
        rows = slice(lower * half, (lower + 1) * half)
        value = own_ref[rows, :]
        for ref in arrived[2 * lower : 2 * lower + 2]:
            value = value + ref[...].astype(F32)
        if attention:
            residual_ref, slot_ref = refs[4:6]
            out_ref, slots_ref = refs[6 + count :]
            value = value + residual_ref[rows, :].astype(F32)
        else:
            out_ref = refs[4 + count]
        out_ref[rows, :] = value.astype(BF16)
    if attention:
        places = lax.broadcasted_iota(jnp.int32, (slots_ref.shape[0], 1), 0)
        pick = (places == slot_ref[...]).astype(F32).astype(BF16)
        slots_ref[...] = jnp.dot(pick, out_ref[...], preferred_element_type=F32).astype(BF16)


def call(kernel, inputs, outs, name, after=()):
    return pl.pallas_call(
        kernel,
        in_specs=[VMEM] * len(inputs) + [ANY] * len(after),
        out_specs=[VMEM] * len(outs),
        out_shape=[jax.ShapeDtypeStruct(shape, dtype) for shape, dtype in outs],
        cost_estimate=COST,
        compiler_params=params(),
        name=name,
    )(*inputs, *after)


def swap(x):
    return lax.ppermute(x, "c", [(0, 1), (1, 0)])


def shift(x, by):
    size = lax.axis_size("x")
    return lax.ppermute(x, "x", [(i, (i + by) % size) for i in range(size)])


def reduce_blocks(x, w_far, w_rest, other_far, other_rest, attention=(), slots=None, middle=None):
    xs = swap(x)
    rows, depth = x.shape
    width = w_far.shape[2]
    half = ((rows // 2, width), BF16)
    half_f32 = ((rows // 2, width), F32)
    far = call(far_kernel, (x, xs, w_far, other_far), [half] * 2, "far_blocks")
    far_up, far_low = shift(far[0], 1), shift(far[1], -1)
    near = call(
        near_kernel,
        (x, xs, w_rest, other_rest, far[0]),
        [half] * 2,
        "near_blocks",
    )
    near_low, near_up = shift(near[0], 1), shift(near[1], -1)
    next_up, next_low, own = call(
        rest_kernel,
        (x, xs, w_rest, other_rest, near[0]),
        [half_f32, half_f32, ((rows, width), F32)],
        "rest_blocks",
    )
    last = call(next_kernel, (next_up, next_low, far_up, far_low), [half] * 2, "next_blocks")
    last_up, last_low = shift(last[0], 1), shift(last[1], -1)
    inputs = [own, near_up, last_up, near_low, last_low]
    outs = [((rows, width), BF16)]
    if attention:
        inputs += attention
        outs.append(((slots, width), BF16))
    between = middle(last[0]) if middle else ()
    kernel = functools.partial(own_kernel, bool(attention), len(between[-1:]))
    return call(kernel, inputs, outs, "own_block", between[-1:]), between


def hidden_kernel(hops, begin, end, features, count, *refs):
    shards = 2 * len(hops)
    x_refs = refs[:shards]
    wg_ref, wu_ref, wr_ref = refs[shards : shards + 3]
    rest = refs[shards + 3 :]
    depth = 2 * x_refs[0].shape[1]
    first_core = lax.axis_index("c") == 0
    sums = None
    if not begin:
        sums, rest = [ref[...] for ref in rest[:4]], rest[4:]
    rest = rest[count:]
    for k, hop in enumerate(hops):
        mine, other = x_refs[2 * k][...], x_refs[2 * k + 1][...]
        x = jnp.concatenate(
            [jnp.where(first_core, mine, other), jnp.where(first_core, other, mine)], axis=1
        )
        start = pl.multiple_of(chip_at(hop) * depth, 128)
        at = 0 if hop == 0 else depth
        rows = pl.ds(start, depth) if begin else slice(at, at + depth)
        wide = x.astype(F32)
        terms = (
            jnp.dot(x, wg_ref[rows, :], preferred_element_type=F32),
            jnp.dot(x, wu_ref[rows, :], preferred_element_type=F32),
            jnp.sum(wide * wide, axis=1, keepdims=True),
            jnp.sum(wide * wr_ref[:, pl.ds(start, depth)], axis=1, keepdims=True),
        )
        sums = terms if sums is None else [a + b for a, b in zip(sums, terms)]
    if not end:
        for ref, value in zip(rest, sums):
            ref[...] = value
        if begin:
            for i, hop in enumerate((0, 2)):
                rows = pl.ds(pl.multiple_of(chip_at(hop) * depth, 128), depth)
                rest[4][i * depth : (i + 1) * depth, :] = wg_ref[rows, :]
                rest[5][i * depth : (i + 1) * depth, :] = wu_ref[rows, :]
        return
    gate, up, squares, logits = sums
    inverse = lax.rsqrt(squares / features + EPSILON)
    scale = inverse / (1.0 + jnp.exp(-logits * inverse))
    gate = gate * scale
    rest[0][...] = (gate / (1.0 + jnp.exp(-gate)) * (up * scale)).astype(BF16)


def hidden_units(shards, hops, weights, begun=(), end=False, after=()):
    rows, width = shards[0].shape
    features, units = weights[2].shape[1], weights[0].shape[1]
    if end:
        outs = [((rows, units), BF16)]
    else:
        outs = [((rows, n), F32) for n in (units, units, 1, 1)]
        outs += [] if begun else [((4 * width, units), BF16)] * 2
    kernel = functools.partial(hidden_kernel, hops, not begun, end, features, len(after))
    return call(kernel, (*shards, *weights, *begun), outs, "hidden", after)


def halves_kernel(behind_ref, ahead_ref, up_ref, low_ref):
    half = up_ref.shape[0]
    up_ref[...] = behind_ref[:half, :]
    low_ref[...] = ahead_ref[half:, :]


def join_kernel(up_ref, low_ref, *refs):
    half = up_ref.shape[0]
    refs[-1][:half, :] = up_ref[...]
    refs[-1][half:, :] = low_ref[...]


def from_slots_kernel(slot_ref, x_ref, out_ref):
    places = lax.broadcasted_iota(jnp.int32, (1, x_ref.shape[0]), 1)
    pick = (slot_ref[...] == places).astype(F32).astype(BF16)
    out_ref[...] = jnp.dot(pick, x_ref[...], preferred_element_type=F32).astype(BF16)


def shards(
    residual, queries, keys, values, lengths, w_out, w_router, expert_ids, w_gate, w_up, w_down
):
    seq_len = queries.shape[0]
    width = residual.shape[1]
    dp_count = lax.axis_size("dp")
    expert_count = w_router.shape[1]
    capacity = 3 * seq_len // (2 * expert_count)
    slots = expert_count * capacity

    same = expert_ids[:, None] == expert_ids[None, :]
    token_at = jnp.arange(seq_len, dtype=jnp.int32)
    rank = jnp.sum((same & (token_at[None, :] < token_at[:, None])).astype(jnp.int32), axis=1)
    slot = expert_ids * capacity + rank

    router = lax.dynamic_index_in_dim(w_router.astype(F32).T, lax.axis_index("dp"), 0)

    w_far, w_rest, other_far, other_rest, token = columns(w_out, width)
    context = attend(lengths, queries, keys, values, token)

    (attended, outgoing), (*down, _) = reduce_blocks(
        context,
        w_far,
        w_rest,
        swap(other_far),
        swap(other_rest),
        [residual, slot.reshape(1, -1)],
        slots,
        lambda done: columns(w_down[0], width, (done,)),
    )
    down[2], down[3] = swap(down[2]), swap(down[3])

    def exchange(x):
        x = x.reshape(dp_count, slots // dp_count, width)
        return lax.all_to_all(x, "dp", split_axis=0, concat_axis=0, tiled=True).reshape(slots, width)

    here = exchange(outgoing)
    behind, ahead = shift(here, 1), shift(here, -1)
    half, full = ((slots // 2, width), BF16), ((slots, width), BF16)
    behind_up, ahead_low = call(halves_kernel, (behind, ahead), [half] * 2, "halves")
    far_up, far_low = shift(behind_up, 1), shift(ahead_low, -1)
    beside = [behind, swap(behind), ahead, swap(ahead)]
    *begun, gate, up = hidden_units(beside, (-1, 1), (w_gate[0], w_up[0], router))
    (far,) = call(join_kernel, (far_up, far_low), [full], "join", (begun[2],))
    weights = (gate, up, router)
    begun = hidden_units([here, swap(here)], (0,), weights, begun, after=(far,))
    (hidden,) = hidden_units([far, swap(far)], (2,), weights, begun, end=True)
    (summed,), _ = reduce_blocks(hidden, *down)
    (expert_out,) = call(
        lambda s, x, o: from_slots_kernel(s, x, o),
        (slot.reshape(-1, 1), exchange(summed)),
        [((seq_len, width), BF16)],
        "from_slots",
    )
    return (attended, expert_out)


def solution(mesh):
    chips = mesh.shape["expert"] // 2
    fine = Mesh(mesh.devices.reshape(mesh.shape["dp"], chips, 2), ("dp", "x", "c"))
    e = ("x", "c")
    in_specs = (
        P("dp", e),
        P("dp", e),
        P("dp", e),
        P("dp", e),
        P(),
        P(e, None),
        P(),
        P("dp"),
        P("dp", None, e),
        P("dp", None, e),
        P("dp", e, None),
    )
    out_specs = (P("dp", e), P("dp", e))
    return jax.shard_map(shards, mesh=fine, in_specs=in_specs, out_specs=out_specs, check_vma=False)
```

time: 185 us -> 175 us (0.946)
  Pallas kernels: 46.8 us -> 34.5 us
  waiting for transfers between devices: 71.2 us -> 75.8 us
    pallas_call x2, Pallas kernels: 13.7 us -> 1.81 us  [columns(): pl.pallas_call(columns_kernel, in_specs=[ANY] * (1 + len(after)), out_spe...]
    ppermute x16, waiting for transfers between devices: 50 us -> 54.6 us  [shift(): return lax.ppermute(x, 'x', [(i, (i + by) % size) for i in range(size)])]
    unnamed x36 -> x38, local copies, waits for them, and re-layouts: 10.1 us -> 9.59 us
    pallas_call x13 -> x16, Pallas kernels: 29 us -> 28.6 us  [call(): pl.pallas_call(kernel, in_specs=[VMEM] * len(inputs) + [ANY] * len(after)...]
    ppermute x9 -> x10, waiting for transfers between devices: 4.79 us -> 4.55 us  [swap(): return lax.ppermute(x, 'c', [(0, 1), (1, 0)])]
  transfers between devices with their start and end apart: 26 -> 27, of which waited for: 14 -> 11; matrix products, arithmetic and copies ran while one was open for 1% -> 1% of each run, Pallas kernels for 19% -> 17%
where the time goes in v2:
time: 175 us; the launch traced here: 174 us
  waiting for transfers between devices  75.8 us (43%)
  Pallas kernels  34.5 us (20%)
  starting transfers between devices  29.9 us (17%)
  blocking collectives  22.3 us (13%)
  local copies, waits for them, and re-layouts  9.74 us (6%)
    ppermute x16, waiting for transfers between devices, shift(): return lax.ppermute(x, 'x', [(i, (i + by) % size) for i in range(size)])  54.6 us
    pallas_call x16, Pallas kernels, call(): pl.pallas_call(kernel, in_specs=[VMEM] * len(inputs) + [ANY] * len(after)...  28.6 us
    ppermute x16, starting transfers between devices, shift(): return lax.ppermute(x, 'x', [(i, (i + by) % size) for i in range(size)])  23.4 us
    all_to_all x1, blocking collectives, exchange(): lax.all_to_all(x, 'dp', split_axis=0, concat_axis=0, tiled=True)  22.3 us
    all_to_all x1, waiting for transfers between devices, exchange(): lax.all_to_all(x, 'dp', split_axis=0, concat_axis=0, tiled=True)  16.7 us
    unnamed x38, local copies, waits for them, and re-layouts  9.59 us
    ppermute x10, waiting for transfers between devices, swap(): return lax.ppermute(x, 'c', [(0, 1), (1, 0)])  4.55 us
    pallas_call x1, Pallas kernels, attend(): pl.pallas_call(functools.partial(attend_kernel, 2), out_shape=jax.ShapeDt...  4.11 us
  transfers between devices with their start and end apart: 27, of which 11 were waited for; matrix products, arithmetic and copies ran while one was open for 1% of the time, Pallas kernels for 17%

profile of v2, /device:TPU:0, one launch (start us, length us, event | category | flops | bytes accessed | tf_op | source)
XLA Modules:
  0.0 174.4 jit_solution(7848969915279846913)
XLA Ops:
  0.6 2.9 %copy-done = bf16[640,5120]{1,0:T(8,128)(2,1)S(1)} copy-done((bf16[640,5120]{1,0:T(8,128)(2,1)S(1)}, bf16[640,5120]{1,0:T(8,128)(2,1)}, u32[]{:S(2)}) %copy-start) | copy-done | bytes 6553624
  3.5 1.0 columns.2
  5.1 4.1 %attend.1.x_ref = bf16[512,640]{1,0:T(8,128)(2,1)S(1)} custom-call(s32[8,16]{1,0:T(8,128)S(1)} %bitcast.25, bf16[512,640]{1,0:T(8,128)(2,1)S(1)} %copy-done.5, bf16[512,128]{1,0:T(8,128)(2,1)S(1)} %copy-done.9, bf16[512,128]{1,0:T(8,128)(2,1)S(1)} %copy-done.10, f32[8,128]{1,0:T(8,128)S(1)} %get-tuple-element.44.after_ref), custom_call_target="tpu_custom_call" | custom-call | flops 1024 | bytes 1024 | tf_op jit(solution)/shard_map/attend/pallas_call | solution.py:108
  9.4 2.0 %collective-permute-done.xs_ref = bf16[512,640]{1,0:T(8,128)(2,1)S(1)} collective-permute-done((bf16[512,640]{1,0:T(8,128)(2,1)S(1)}, bf16[512,640]{1,0:T(8,128)(2,1)S(1)}, u32[]{:S(2)}, u32[]{:S(2)}) %collective-permute-start) | collective-permute-done | bytes 655392 | tf_op jit(solution)/shard_map/ppermute | solution.py:185
  11.4 1.3 far_blocks.2
  12.7 1.6 collective-permute-start.4
  14.4 1.7 collective-permute-start.5
  16.0 1.3 near_blocks.2
  17.8 2.5 %rest_blocks.2 = (f32[256,640]{1,0:T(8,128)S(1)}, f32[256,640]{1,0:T(8,128)S(1)}, f32[512,640]{1,0:T(8,128)S(1)}) custom-call(bf16[512,640]{1,0:T(8,128)(2,1)S(1)} %attend.1.x_ref, bf16[512,640]{1,0:T(8,128)(2,1)S(1)} %collective-permute-done.xs_ref, bf16[3,640,640]{2,1,0:T(8,128)(2,1)S(1)} %get-tuple-element.45.w_ref, ...), custom_call_target="tpu_custom_call" | custom-call | flops 1024 | bytes 1024 | tf_op jit(solution)/shard_map/rest_blocks/pallas_call | solution.py:173
  20.3 4.3 %collective-permute-done.4.far_up = bf16[256,640]{1,0:T(8,128)(2,1)S(1)} collective-permute-done((bf16[256,640]{1,0:T(8,128)(2,1)S(1)}, bf16[256,640]{1,0:T(8,128)(2,1)S(1)}, u32[]{:S(2)}, u32[]{:S(2)}) %collective-permute-start.4) | collective-permute-done | bytes 327712 | tf_op jit(solution)/shard_map/ppermute | solution.py:190
  24.7 0.8 collective-permute-start.6
  25.5 2.5 %collective-permute-start.8 = (bf16[256,640]{1,0:T(8,128)(2,1)S(1)}, bf16[256,640]{1,0:T(8,128)(2,1)S(1)}, u32[]{:S(2)}, u32[]{:S(2)}) collective-permute-start(bf16[256,640]{1,0:T(8,128)(2,1)S(1)} %get-tuple-element.57), channel_id=1, source_target_pairs={{0,6},{2,0},{4,2},{6,4},{1,7},{3,1},{5,3},{7,5},{8,14},{10,8},{12,... | collective-permute-start | bytes 983048 | tf_op jit(solution)/shard_map/ppermute | solution.py:190
  28.0 0.9 collective-permute-start.3
  29.2 0.8 columns.3
  30.1 1.3 copy-done.12
  31.4 6.4 %collective-permute-done.6.refs_1_ = bf16[256,640]{1,0:T(8,128)(2,1)S(1)} collective-permute-done((bf16[256,640]{1,0:T(8,128)(2,1)S(1)}, bf16[256,640]{1,0:T(8,128)(2,1)S(1)}, u32[]{:S(2)}, u32[]{:S(2)}) %collective-permute-start.6) | collective-permute-done | bytes 327712 | tf_op jit(solution)/shard_map/ppermute | solution.py:190
  37.8 3.1 %collective-permute-done.3.refs_0_ = bf16[256,640]{1,0:T(8,128)(2,1)S(1)} collective-permute-done((bf16[256,640]{1,0:T(8,128)(2,1)S(1)}, bf16[256,640]{1,0:T(8,128)(2,1)S(1)}, u32[]{:S(2)}, u32[]{:S(2)}) %collective-permute-start.3) | collective-permute-done | bytes 327712 | tf_op jit(solution)/shard_map/ppermute | solution.py:190
  40.9 1.4 own_block.2
  42.3 22.3 %all_to_all.10 = bf16[16,48,640]{2,1,0:T(8,128)(2,1)S(1)} all-to-all(bf16[16,48,640]{2,1,0:T(8,128)(2,1)S(1)} %bitcast.22), channel_id=1, replica_groups=mesh['dp'=16,'x'=4,'c'=2] {'dp'}, dimensions={0} | all-to-all | bytes 1966080 | tf_op jit(solution)/shard_map/all_to_all | solution.py:333
  64.6 1.3 collective-permute-start.9
  65.8 2.0 %collective-permute-start.10 = (bf16[768,640]{1,0:T(8,128)(2,1)S(1)}, bf16[768,640]{1,0:T(8,128)(2,1)}, u32[]{:S(2)}, u32[]{:S(2)}) collective-permute-start(bf16[768,640]{1,0:T(8,128)(2,1)S(1)} %bitcast.19), channel_id=1, source_target_pairs={{0,6},{2,0},{4,2},{6,4},{1,7},{3,1},{5,3},{7,5},{8,14},{10,8},{12,... | collective-permute-start | bytes 2949128 | tf_op jit(solution)/shard_map/ppermute | solution.py:190
  67.9 18.0 %collective-permute-done.9.behind_ref.refs_0_ = bf16[768,640]{1,0:T(8,128)(2,1)S(1)} collective-permute-done((bf16[768,640]{1,0:T(8,128)(2,1)S(1)}, bf16[768,640]{1,0:T(8,128)(2,1)S(1)}, u32[]{:S(2)}, u32[]{:S(2)}) %collective-permute-start.9) | collective-permute-done | bytes 983072 | tf_op jit(solution)/shard_map/ppermute | solution.py:190
  85.9 0.5 collective-permute-start.14
  86.4 1.3 halves.1
  87.6 1.1 collective-permute-start.11
  88.7 2.3 %collective-permute-start.12 = (bf16[384,640]{1,0:T(8,128)(2,1)S(1)}, bf16[384,640]{1,0:T(8,128)(2,1)S(1)}, u32[]{:S(2)}, u32[]{:S(2)}) collective-permute-start(bf16[384,640]{1,0:T(8,128)(2,1)S(1)} %get-tuple-element.62), channel_id=1, source_target_pairs={{0,6},{2,0},{4,2},{6,4},{1,7},{3,1},{5,3},{7,5},{8,14},{10,8},{12,... | collective-permute-start | bytes 1474568 | tf_op jit(solution)/shard_map/ppermute | solution.py:190
  91.0 0.9 fusion.1.refs_6_.refs_4_
  92.0 2.5 %copy-done.1 = bf16[1,5120,512]{2,1,0:T(8,128)(2,1)S(1)} copy-done((bf16[1,5120,512]{2,1,0:T(8,128)(2,1)S(1)}, bf16[1,5120,512]{2,1,0:T(8,128)(2,1)}, u32[]{:S(2)}) %copy-start.1) | copy-done | bytes 5242904
  94.5 2.5 %copy-done.2 = bf16[1,5120,512]{2,1,0:T(8,128)(2,1)S(1)} copy-done((bf16[1,5120,512]{2,1,0:T(8,128)(2,1)S(1)}, bf16[1,5120,512]{2,1,0:T(8,128)(2,1)}, u32[]{:S(2)}) %copy-start.2) | copy-done | bytes 5242904
  97.0 6.9 %hidden.3 = (f32[768,512]{1,0:T(8,128)S(1)}, f32[768,512]{1,0:T(8,128)S(1)}, f32[768,1]{1,0:T(8,128)S(1)}, f32[768,1]{1,0:T(8,128)S(1)}, bf16[2560,512]{1,0:T(8,128)(2,1)S(1)}, /*index=5*/bf16[2560,512]{1,0:T(8,128)(2,1)S(1)}) custom-call(bf16[768,640]{1,0:T(8,128)(2,1)S(1)} %collective-permute-done.9.behind_ref.refs_0_, ...), custom_call_target="tpu_custom_call" | custom-call | flops 1024 | bytes 1024 | tf_op jit(solution)/shard_map/hidden/pallas_call | solution.py:173
  103.9 0.6 collective-permute-start.15
  105.0 2.6 %hidden.4 = (f32[768,512]{1,0:T(8,128)S(1)}, f32[768,512]{1,0:T(8,128)S(1)}, f32[768,1]{1,0:T(8,128)S(1)}, f32[768,1]{1,0:T(8,128)S(1)}) custom-call(bf16[768,640]{1,0:T(8,128)(2,1)S(1)} %bitcast.21, bf16[768,640]{1,0:T(8,128)(2,1)S(1)} %collective-permute-done.16.refs_1_, bf16[2560,512]{1,0:T(8,128)(2,1)S(1)} %get-tuple-element.64.refs_2_, ...), custom_call_target="tpu_custom_call" | custom-call | flops 1024 | bytes 1024 | tf_op jit(solution)/shard_map/hidden/pallas_call | solution.py:173
  107.6 2.7 %hidden.5.x_ref = bf16[768,512]{1,0:T(8,128)(2,1)S(1)} custom-call(bf16[768,640]{1,0:T(8,128)(2,1)S(1)} %join.1.refs_9_.refs_0_, bf16[768,640]{1,0:T(8,128)(2,1)S(1)} %collective-permute-done.15.refs_1_, bf16[2560,512]{1,0:T(8,128)(2,1)S(1)} %get-tuple-element.64.refs_2_, bf16[2560,512]{1,0:T(8,128)(2,1)S(1)} %get-tuple-element.65.refs_3_, ...), custom_call_target="tpu_custom_call" | custom-call | flops 1024 | bytes 1024 | tf_op jit(solution)/shard_map/hidden/pallas_call | solution.py:173
  110.3 0.6 collective-permute-start.17
  111.2 2.5 %collective-permute-done.19.ws_ref = bf16[1,512,640]{2,1,0:T(8,128)(2,1)S(1)} collective-permute-done((bf16[1,512,640]{2,1,0:T(8,128)(2,1)S(1)}, bf16[1,512,640]{2,1,0:T(8,128)(2,1)S(1)}, u32[]{:S(2)}, u32[]{:S(2)}) %collective-permute-start.19) | collective-permute-done | bytes 655392 | tf_op jit(solution)/shard_map/ppermute | solution.py:185
  113.7 1.4 far_blocks.3
  115.2 3.2 %collective-permute-start.22 = (bf16[384,640]{1,0:T(8,128)(2,1)S(1)}, bf16[384,640]{1,0:T(8,128)(2,1)S(1)}, u32[]{:S(2)}, u32[]{:S(2)}) collective-permute-start(bf16[384,640]{1,0:T(8,128)(2,1)S(1)} %get-tuple-element.83), channel_id=1, source_target_pairs={{0,6},{2,0},{4,2},{6,4},{1,7},{3,1},{5,3},{7,5},{8,14},{10,8},{12,... | collective-permute-start | bytes 1474568 | tf_op jit(solution)/shard_map/ppermute | solution.py:190
  118.4 1.4 near_blocks.3
  120.0 1.9 %collective-permute-start.24 = (bf16[384,640]{1,0:T(8,128)(2,1)S(1)}, bf16[384,640]{1,0:T(8,128)(2,1)S(1)}, u32[]{:S(2)}, u32[]{:S(2)}) collective-permute-start(bf16[384,640]{1,0:T(8,128)(2,1)S(1)} %get-tuple-element.78.after_ref), channel_id=1, source_target_pairs={{0,2},{2,4},{4,6},{6,0},{1,3},{3,5},{5,7},{7,1},{8,10},{10,12},{12... | collective-permute-start | bytes 1474568 | tf_op jit(solution)/shard_map/ppermute | solution.py:190
  121.9 2.6 %rest_blocks.3 = (f32[384,640]{1,0:T(8,128)S(1)}, f32[384,640]{1,0:T(8,128)S(1)}, f32[768,640]{1,0:T(8,128)S(1)}) custom-call(bf16[768,512]{1,0:T(8,128)(2,1)S(1)} %hidden.5.x_ref, bf16[768,512]{1,0:T(8,128)(2,1)S(1)} %collective-permute-done.17.xs_ref, bf16[3,512,640]{2,1,0:T(8,128)(2,1)S(1)} %get-tuple-element.73.w_ref, ...), custom_call_target="tpu_custom_call" | custom-call | flops 1024 | bytes 1024 | tf_op jit(solution)/shard_map/rest_blocks/pallas_call | solution.py:173
  124.5 5.9 %collective-permute-done.21.far_up = bf16[384,640]{1,0:T(8,128)(2,1)S(1)} collective-permute-done((bf16[384,640]{1,0:T(8,128)(2,1)S(1)}, bf16[384,640]{1,0:T(8,128)(2,1)S(1)}, u32[]{:S(2)}, u32[]{:S(2)}) %collective-permute-start.21) | collective-permute-done | bytes 491552 | tf_op jit(solution)/shard_map/ppermute | solution.py:190
  130.7 3.3 %collective-permute-start.25 = (bf16[384,640]{1,0:T(8,128)(2,1)S(1)}, bf16[384,640]{1,0:T(8,128)(2,1)S(1)}, u32[]{:S(2)}, u32[]{:S(2)}) collective-permute-start(bf16[384,640]{1,0:T(8,128)(2,1)S(1)} %get-tuple-element.85), channel_id=1, source_target_pairs={{0,6},{2,0},{4,2},{6,4},{1,7},{3,1},{5,3},{7,5},{8,14},{10,8},{12,... | collective-permute-start | bytes 1474568 | tf_op jit(solution)/shard_map/ppermute | solution.py:190
  134.0 6.5 %collective-permute-done.20.refs_0_ = bf16[384,640]{1,0:T(8,128)(2,1)S(1)} collective-permute-done((bf16[384,640]{1,0:T(8,128)(2,1)S(1)}, bf16[384,640]{1,0:T(8,128)(2,1)S(1)}, u32[]{:S(2)}, u32[]{:S(2)}) %collective-permute-start.20) | collective-permute-done | bytes 491552 | tf_op jit(solution)/shard_map/ppermute | solution.py:190
  141.0 10.0 %collective-permute-done.23.refs_1_ = bf16[384,640]{1,0:T(8,128)(2,1)S(1)} collective-permute-done((bf16[384,640]{1,0:T(8,128)(2,1)S(1)}, bf16[384,640]{1,0:T(8,128)(2,1)S(1)}, u32[]{:S(2)}, u32[]{:S(2)}) %collective-permute-start.23) | collective-permute-done | bytes 491552 | tf_op jit(solution)/shard_map/ppermute | solution.py:190
  151.0 1.3 own_block.3
  152.2 3.6 %all-to-all-start.1 = ((bf16[16,48,640]{2,1,0:T(8,128)(2,1)}), bf16[16,48,640]{2,1,0:T(8,128)(2,1)S(1)}, u32[]{:S(2)}, u32[]{:S(2)}) async-start(bf16[16,48,640]{2,1,0:T(8,128)(2,1)} %bitcast.9), calls=%async_computation.1 | async-start | bytes 1966080 | tf_op jit(solution)/shard_map/all_to_all | solution.py:333
  156.0 16.7 %all-to-all-done.1 = bf16[16,48,640]{2,1,0:T(8,128)(2,1)S(1)} async-done(((bf16[16,48,640]{2,1,0:T(8,128)(2,1)}), bf16[16,48,640]{2,1,0:T(8,128)(2,1)S(1)}, u32[]{:S(2)}, u32[]{:S(2)}) %all-to-all-start.1) | async-done | bytes 983072 | tf_op jit(solution)/shard_map/all_to_all | solution.py:333
  172.7 1.7 from_slots.1
  (69 shorter events, 3.8 us)
Async XLA Ops:
  0.6 2.9 %copy-start = (bf16[640,5120]{1,0:T(8,128)(2,1)S(1)}, bf16[640,5120]{1,0:T(8,128)(2,1)}, u32[]{:S(2)}) copy-start(bf16[640,5120]{1,0:T(8,128)(2,1)} %w_ref.1) | copy-start | bytes 19660804
  3.5 1.6 copy-start.5
  3.5 1.6 copy-start.9
  3.5 1.6 copy-start.10
  3.5 1.6 copy-start.11
  4.5 11.5 %collective-permute-start.1 = (bf16[3,640,640]{2,1,0:T(8,128)(2,1)S(1)}, bf16[3,640,640]{2,1,0:T(8,128)(2,1)S(1)}, u32[]{:S(2)}, u32[]{:S(2)}) collective-permute-start(bf16[3,640,640]{2,1,0:T(8,128)(2,1)S(1)} %get-tuple-element.46), channel_id=1, source_target_pairs={{0,1},{1,0},{2,3},{3,2},{4,5},{5,4},{6,7},{7,6},{8,9},{9,8},{10,11... | collective-permute-start | bytes 7372808 | tf_op jit(solution)/shard_map/ppermute | solution.py:185
  4.6 6.8 %collective-permute-start.2 = (bf16[1,640,640]{2,1,0:T(8,128)(2,1)S(1)}, bf16[1,640,640]{2,1,0:T(8,128)(2,1)S(1)}, u32[]{:S(2)}, u32[]{:S(2)}) collective-permute-start(bf16[1,640,640]{2,1,0:T(8,128)(2,1)S(1)} %get-tuple-element.48), channel_id=1, source_target_pairs={{0,1},{1,0},{2,3},{3,2},{4,5},{5,4},{6,7},{7,6},{8,9},{9,8},{10,11... | collective-permute-start | bytes 2457608 | tf_op jit(solution)/shard_map/ppermute | solution.py:185
  9.2 2.2 %collective-permute-start = (bf16[512,640]{1,0:T(8,128)(2,1)S(1)}, bf16[512,640]{1,0:T(8,128)(2,1)S(1)}, u32[]{:S(2)}, u32[]{:S(2)}) collective-permute-start(bf16[512,640]{1,0:T(8,128)(2,1)S(1)} %attend.1.x_ref), channel_id=1, source_target_pairs={{0,1},{1,0},{2,3},{3,2},{4,5},{5,4},{6,7},{7,6},{8,9},{9,8},{10,11... | collective-permute-start | bytes 1966088 | tf_op jit(solution)/shard_map/ppermute | solution.py:185
  12.7 11.8 %collective-permute-start.4 = (bf16[256,640]{1,0:T(8,128)(2,1)S(1)}, bf16[256,640]{1,0:T(8,128)(2,1)S(1)}, u32[]{:S(2)}, u32[]{:S(2)}) collective-permute-start(bf16[256,640]{1,0:T(8,128)(2,1)S(1)} %get-tuple-element.49.after_ref), channel_id=1, source_target_pairs={{0,2},{2,4},{4,6},{6,0},{1,3},{3,5},{5,7},{7,1},{8,10},{10,12},{12... | collective-permute-start | bytes 983048 | tf_op jit(solution)/shard_map/ppermute | solution.py:190
  14.4 10.2 %collective-permute-start.5 = (bf16[256,640]{1,0:T(8,128)(2,1)S(1)}, bf16[256,640]{1,0:T(8,128)(2,1)S(1)}, u32[]{:S(2)}, u32[]{:S(2)}) collective-permute-start(bf16[256,640]{1,0:T(8,128)(2,1)S(1)} %get-tuple-element.55), channel_id=1, source_target_pairs={{0,6},{2,0},{4,2},{6,4},{1,7},{3,1},{5,3},{7,5},{8,14},{10,8},{12,... | collective-permute-start | bytes 983048 | tf_op jit(solution)/shard_map/ppermute | solution.py:190
  16.0 13.2 %slice-start = ((s8[5242880]{0:T(1024)(128)(4,1)}), s8[4194304]{0:T(1024)(128)(4,1)S(1)}, s32[]{:S(2)}) async-start(s8[5242880]{0:T(1024)(128)(4,1)} %bitcast.14), calls=%async_computation.2 | async-start | bytes 8388608
  17.4 11.6 %copy-start.16 = (s32[512]{0:T(512)S(1)}, s32[512]{0:T(512)}, u32[]{:S(2)}) copy-start(s32[512]{0:T(512)} %param.18) | copy-start | bytes 6148
  17.4 11.8 %slice-start.1 = ((s8[5242880]{0:T(1024)(128)(4,1)}), s8[1048576]{0:T(1024)(128)(4,1)S(1)}, s32[]{:S(2)}) async-start(s8[5242880]{0:T(1024)(128)(4,1)} %bitcast.14), calls=%async_computation.3 | async-start | bytes 2097152
  17.4 20.4 %collective-permute-start.7 = (bf16[256,640]{1,0:T(8,128)(2,1)S(1)}, bf16[256,640]{1,0:T(8,128)(2,1)S(1)}, u32[]{:S(2)}, u32[]{:S(2)}) collective-permute-start(bf16[256,640]{1,0:T(8,128)(2,1)S(1)} %get-tuple-element.50.after_ref), channel_id=1, source_target_pairs={{0,2},{2,4},{4,6},{6,0},{1,3},{3,5},{5,7},{7,1},{8,10},{10,12},{12... | collective-permute-start | bytes 983048 | tf_op jit(solution)/shard_map/ppermute | solution.py:190
  24.7 13.1 %collective-permute-start.6 = (bf16[256,640]{1,0:T(8,128)(2,1)S(1)}, bf16[256,640]{1,0:T(8,128)(2,1)S(1)}, u32[]{:S(2)}, u32[]{:S(2)}) collective-permute-start(bf16[256,640]{1,0:T(8,128)(2,1)S(1)} %get-tuple-element.56.refs_0_), channel_id=1, source_target_pairs={{0,2},{2,4},{4,6},{6,0},{1,3},{3,5},{5,7},{7,1},{8,10},{10,12},{12... | collective-permute-start | bytes 983048 | tf_op jit(solution)/shard_map/ppermute | solution.py:190
  25.5 12.3 %collective-permute-start.8 = (bf16[256,640]{1,0:T(8,128)(2,1)S(1)}, bf16[256,640]{1,0:T(8,128)(2,1)S(1)}, u32[]{:S(2)}, u32[]{:S(2)}) collective-permute-start(bf16[256,640]{1,0:T(8,128)(2,1)S(1)} %get-tuple-element.57), channel_id=1, source_target_pairs={{0,6},{2,0},{4,2},{6,4},{1,7},{3,1},{5,3},{7,5},{8,14},{10,8},{12,... | collective-permute-start | bytes 983048 | tf_op jit(solution)/shard_map/ppermute | solution.py:190
  28.0 12.9 %collective-permute-start.3 = (bf16[256,640]{1,0:T(8,128)(2,1)S(1)}, bf16[256,640]{1,0:T(8,128)(2,1)S(1)}, u32[]{:S(2)}, u32[]{:S(2)}) collective-permute-start(bf16[256,640]{1,0:T(8,128)(2,1)S(1)} %get-tuple-element.52), channel_id=1, source_target_pairs={{0,6},{2,0},{4,2},{6,4},{1,7},{3,1},{5,3},{7,5},{8,14},{10,8},{12,... | collective-permute-start | bytes 983048 | tf_op jit(solution)/shard_map/ppermute | solution.py:190
  29.2 11.7 %copy-start.6 = (bf16[512,640]{1,0:T(8,128)(2,1)S(1)}, bf16[512,640]{1,0:T(8,128)(2,1)}, u32[]{:S(2)}) copy-start(bf16[512,640]{1,0:T(8,128)(2,1)} %refs_4_.1) | copy-start | bytes 1966084
  30.1 1.3 copy-start.12
  31.4 33.2 %copy-start.7 = (bf16[1,512,640]{2,1,0:T(8,128)(2,1)}, bf16[1,512,640]{2,1,0:T(8,128)(2,1)S(1)}, u32[]{:S(2)}) copy-start(bf16[1,512,640]{2,1,0:T(8,128)(2,1)S(1)} %get-tuple-element.75.w_ref) | copy-start | bytes 1966084
  31.4 33.2 %copy-start.14 = (bf16[1,512,640]{2,1,0:T(8,128)(2,1)}, bf16[1,512,640]{2,1,0:T(8,128)(2,1)S(1)}, u32[]{:S(2)}) copy-start(bf16[1,512,640]{2,1,0:T(8,128)(2,1)S(1)} %get-tuple-element.76) | copy-start | bytes 1966084
  64.6 21.3 %copy-start.3 = (bf16[16,48,640]{2,1,0:T(8,128)(2,1)}, bf16[16,48,640]{2,1,0:T(8,128)(2,1)S(1)}, u32[]{:S(2)}) copy-start(bf16[16,48,640]{2,1,0:T(8,128)(2,1)S(1)} %all_to_all.10) | copy-start | bytes 2949124
  64.6 21.3 %collective-permute-start.9 = (bf16[768,640]{1,0:T(8,128)(2,1)S(1)}, bf16[768,640]{1,0:T(8,128)(2,1)S(1)}, u32[]{:S(2)}, u32[]{:S(2)}) collective-permute-start(bf16[768,640]{1,0:T(8,128)(2,1)S(1)} %bitcast.18), channel_id=1, source_target_pairs={{0,2},{2,4},{4,6},{6,0},{1,3},{3,5},{5,7},{7,1},{8,10},{10,12},{12... | collective-permute-start | bytes 2949128 | tf_op jit(solution)/shard_map/ppermute | solution.py:190
  65.8 20.0 %collective-permute-start.10 = (bf16[768,640]{1,0:T(8,128)(2,1)S(1)}, bf16[768,640]{1,0:T(8,128)(2,1)}, u32[]{:S(2)}, u32[]{:S(2)}) collective-permute-start(bf16[768,640]{1,0:T(8,128)(2,1)S(1)} %bitcast.19), channel_id=1, source_target_pairs={{0,6},{2,0},{4,2},{6,4},{1,7},{3,1},{5,3},{7,5},{8,14},{10,8},{12,... | collective-permute-start | bytes 2949128 | tf_op jit(solution)/shard_map/ppermute | solution.py:190
  85.9 6.1 %collective-permute-start.13 = (bf16[768,640]{1,0:T(8,128)(2,1)S(1)}, bf16[768,640]{1,0:T(8,128)(2,1)}, u32[]{:S(2)}, u32[]{:S(2)}) collective-permute-start(bf16[768,640]{1,0:T(8,128)(2,1)S(1)} %collective-permute-done.9.behind_ref.refs_0_), channel_id=1, source_target_pairs={{0,1},{1,0},{2,3},{3,2},{4,5},{5,4},{6,7},{7,6},{8,9},{9,8},{10,11... | collective-permute-start | bytes 2949128 | tf_op jit(solution)/shard_map/ppermute | solution.py:185
  85.9 6.1 %collective-permute-start.14 = (bf16[768,640]{1,0:T(8,128)(2,1)}, bf16[768,640]{1,0:T(8,128)(2,1)}, u32[]{:S(2)}, u32[]{:S(2)}) collective-permute-start(bf16[768,640]{1,0:T(8,128)(2,1)} %collective-permute-done.10.ahead_ref.refs_2_), channel_id=1, source_target_pairs={{0,1},{1,0},{2,3},{3,2},{4,5},{5,4},{6,7},{7,6},{8,9},{9,8},{10,11... | collective-permute-start | bytes 2949128 | tf_op jit(solution)/shard_map/ppermute | solution.py:185
  87.6 16.2 %collective-permute-start.11 = (bf16[384,640]{1,0:T(8,128)(2,1)S(1)}, bf16[384,640]{1,0:T(8,128)(2,1)S(1)}, u32[]{:S(2)}, u32[]{:S(2)}) collective-permute-start(bf16[384,640]{1,0:T(8,128)(2,1)S(1)} %get-tuple-element.61), channel_id=1, source_target_pairs={{0,2},{2,4},{4,6},{6,0},{1,3},{3,5},{5,7},{7,1},{8,10},{10,12},{12... | collective-permute-start | bytes 1474568 | tf_op jit(solution)/shard_map/ppermute | solution.py:190
  88.7 15.1 %collective-permute-start.12 = (bf16[384,640]{1,0:T(8,128)(2,1)S(1)}, bf16[384,640]{1,0:T(8,128)(2,1)S(1)}, u32[]{:S(2)}, u32[]{:S(2)}) collective-permute-start(bf16[384,640]{1,0:T(8,128)(2,1)S(1)} %get-tuple-element.62), channel_id=1, source_target_pairs={{0,6},{2,0},{4,2},{6,4},{1,7},{3,1},{5,3},{7,5},{8,14},{10,8},{12,... | collective-permute-start | bytes 1474568 | tf_op jit(solution)/shard_map/ppermute | solution.py:190
  91.9 12.7 %collective-permute-start.16 = (bf16[768,640]{1,0:T(8,128)(2,1)}, bf16[768,640]{1,0:T(8,128)(2,1)S(1)}, u32[]{:S(2)}, u32[]{:S(2)}) collective-permute-start(bf16[768,640]{1,0:T(8,128)(2,1)} %bitcast.20), channel_id=1, source_target_pairs={{0,1},{1,0},{2,3},{3,2},{4,5},{5,4},{6,7},{7,6},{8,9},{9,8},{10,11... | collective-permute-start | bytes 2949128 | tf_op jit(solution)/shard_map/ppermute | solution.py:185
  92.0 2.5 %copy-start.1 = (bf16[1,5120,512]{2,1,0:T(8,128)(2,1)S(1)}, bf16[1,5120,512]{2,1,0:T(8,128)(2,1)}, u32[]{:S(2)}) copy-start(bf16[1,5120,512]{2,1,0:T(8,128)(2,1)} %param.19) | copy-start | bytes 15728644
  94.5 2.5 %copy-start.2 = (bf16[1,5120,512]{2,1,0:T(8,128)(2,1)S(1)}, bf16[1,5120,512]{2,1,0:T(8,128)(2,1)}, u32[]{:S(2)}) copy-start(bf16[1,5120,512]{2,1,0:T(8,128)(2,1)} %param.20) | copy-start | bytes 15728644
  97.0 7.6 %copy-start.13 = (bf16[3,512,640]{2,1,0:T(8,128)(2,1)S(1)}, bf16[3,512,640]{2,1,0:T(8,128)(2,1)}, u32[]{:S(2)}) copy-start(bf16[3,512,640]{2,1,0:T(8,128)(2,1)} %copy-done.12) | copy-start | bytes 5898244
  103.8 1.2 copy-start.4
  103.9 3.7 %collective-permute-start.15 = (bf16[768,640]{1,0:T(8,128)(2,1)S(1)}, bf16[768,640]{1,0:T(8,128)(2,1)S(1)}, u32[]{:S(2)}, u32[]{:S(2)}) collective-permute-start(bf16[768,640]{1,0:T(8,128)(2,1)S(1)} %join.1.refs_9_.refs_0_), channel_id=1, source_target_pairs={{0,1},{1,0},{2,3},{3,2},{4,5},{5,4},{6,7},{7,6},{8,9},{9,8},{10,11... | collective-permute-start | bytes 2949128 | tf_op jit(solution)/shard_map/ppermute | solution.py:185
  104.5 13.9 %collective-permute-start.18 = (bf16[3,512,640]{2,1,0:T(8,128)(2,1)S(1)}, bf16[3,512,640]{2,1,0:T(8,128)(2,1)S(1)}, u32[]{:S(2)}, u32[]{:S(2)}) collective-permute-start(bf16[3,512,640]{2,1,0:T(8,128)(2,1)S(1)} %copy-done.13), channel_id=1, source_target_pairs={{0,1},{1,0},{2,3},{3,2},{4,5},{5,4},{6,7},{7,6},{8,9},{9,8},{10,11... | collective-permute-start | bytes 5898248 | tf_op jit(solution)/shard_map/ppermute | solution.py:185
  107.6 3.3 %copy-start.15 = (bf16[1,512,640]{2,1,0:T(8,128)(2,1)S(1)}, bf16[1,512,640]{2,1,0:T(8,128)(2,1)}, u32[]{:S(2)}) copy-start(bf16[1,512,640]{2,1,0:T(8,128)(2,1)} %copy-done.14) | copy-start | bytes 1966084
  107.6 6.1 %copy-start.8 = (bf16[1,512,640]{2,1,0:T(8,128)(2,1)S(1)}, bf16[1,512,640]{2,1,0:T(8,128)(2,1)}, u32[]{:S(2)}) copy-start(bf16[1,512,640]{2,1,0:T(8,128)(2,1)} %copy-done.7) | copy-start | bytes 1966084
  110.3 3.4 %collective-permute-start.17 = (bf16[768,512]{1,0:T(8,128)(2,1)S(1)}, bf16[768,512]{1,0:T(8,128)(2,1)S(1)}, u32[]{:S(2)}, u32[]{:S(2)}) collective-permute-start(bf16[768,512]{1,0:T(8,128)(2,1)S(1)} %hidden.5.x_ref), channel_id=1, source_target_pairs={{0,1},{1,0},{2,3},{3,2},{4,5},{5,4},{6,7},{7,6},{8,9},{9,8},{10,11... | collective-permute-start | bytes 2359304 | tf_op jit(solution)/shard_map/ppermute | solution.py:185
  110.9 2.8 %collective-permute-start.19 = (bf16[1,512,640]{2,1,0:T(8,128)(2,1)S(1)}, bf16[1,512,640]{2,1,0:T(8,128)(2,1)S(1)}, u32[]{:S(2)}, u32[]{:S(2)}) collective-permute-start(bf16[1,512,640]{2,1,0:T(8,128)(2,1)S(1)} %copy-done.15), channel_id=1, source_target_pairs={{0,1},{1,0},{2,3},{3,2},{4,5},{5,4},{6,7},{7,6},{8,9},{9,8},{10,11... | collective-permute-start | bytes 1966088 | tf_op jit(solution)/shard_map/ppermute | solution.py:185
  115.1 15.3 %collective-permute-start.21 = (bf16[384,640]{1,0:T(8,128)(2,1)S(1)}, bf16[384,640]{1,0:T(8,128)(2,1)S(1)}, u32[]{:S(2)}, u32[]{:S(2)}) collective-permute-start(bf16[384,640]{1,0:T(8,128)(2,1)S(1)} %get-tuple-element.77.after_ref), channel_id=1, source_target_pairs={{0,2},{2,4},{4,6},{6,0},{1,3},{3,5},{5,7},{7,1},{8,10},{10,12},{12... | collective-permute-start | bytes 1474568 | tf_op jit(solution)/shard_map/ppermute | solution.py:190
  115.2 15.3 %collective-permute-start.22 = (bf16[384,640]{1,0:T(8,128)(2,1)S(1)}, bf16[384,640]{1,0:T(8,128)(2,1)S(1)}, u32[]{:S(2)}, u32[]{:S(2)}) collective-permute-start(bf16[384,640]{1,0:T(8,128)(2,1)S(1)} %get-tuple-element.83), channel_id=1, source_target_pairs={{0,6},{2,0},{4,2},{6,4},{1,7},{3,1},{5,3},{7,5},{8,14},{10,8},{12,... | collective-permute-start | bytes 1474568 | tf_op jit(solution)/shard_map/ppermute | solution.py:190
  119.8 20.7 %collective-permute-start.20 = (bf16[384,640]{1,0:T(8,128)(2,1)S(1)}, bf16[384,640]{1,0:T(8,128)(2,1)S(1)}, u32[]{:S(2)}, u32[]{:S(2)}) collective-permute-start(bf16[384,640]{1,0:T(8,128)(2,1)S(1)} %get-tuple-element.80), channel_id=1, source_target_pairs={{0,6},{2,0},{4,2},{6,4},{1,7},{3,1},{5,3},{7,5},{8,14},{10,8},{12,... | collective-permute-start | bytes 1474568 | tf_op jit(solution)/shard_map/ppermute | solution.py:190
  120.0 20.9 %collective-permute-start.24 = (bf16[384,640]{1,0:T(8,128)(2,1)S(1)}, bf16[384,640]{1,0:T(8,128)(2,1)S(1)}, u32[]{:S(2)}, u32[]{:S(2)}) collective-permute-start(bf16[384,640]{1,0:T(8,128)(2,1)S(1)} %get-tuple-element.78.after_ref), channel_id=1, source_target_pairs={{0,2},{2,4},{4,6},{6,0},{1,3},{3,5},{5,7},{7,1},{8,10},{10,12},{12... | collective-permute-start | bytes 1474568 | tf_op jit(solution)/shard_map/ppermute | solution.py:190
  130.6 20.3 %collective-permute-start.23 = (bf16[384,640]{1,0:T(8,128)(2,1)S(1)}, bf16[384,640]{1,0:T(8,128)(2,1)S(1)}, u32[]{:S(2)}, u32[]{:S(2)}) collective-permute-start(bf16[384,640]{1,0:T(8,128)(2,1)S(1)} %get-tuple-element.84), channel_id=1, source_target_pairs={{0,2},{2,4},{4,6},{6,0},{1,3},{3,5},{5,7},{7,1},{8,10},{10,12},{12... | collective-permute-start | bytes 1474568 | tf_op jit(solution)/shard_map/ppermute | solution.py:190
  130.7 20.3 %collective-permute-start.25 = (bf16[384,640]{1,0:T(8,128)(2,1)S(1)}, bf16[384,640]{1,0:T(8,128)(2,1)S(1)}, u32[]{:S(2)}, u32[]{:S(2)}) collective-permute-start(bf16[384,640]{1,0:T(8,128)(2,1)S(1)} %get-tuple-element.85), channel_id=1, source_target_pairs={{0,6},{2,0},{4,2},{6,4},{1,7},{3,1},{5,3},{7,5},{8,14},{10,8},{12,... | collective-permute-start | bytes 1474568 | tf_op jit(solution)/shard_map/ppermute | solution.py:190
  152.2 20.5 %all-to-all-start.1 = ((bf16[16,48,640]{2,1,0:T(8,128)(2,1)}), bf16[16,48,640]{2,1,0:T(8,128)(2,1)S(1)}, u32[]{:S(2)}, u32[]{:S(2)}) async-start(bf16[16,48,640]{2,1,0:T(8,128)(2,1)} %bitcast.9), calls=%async_computation.1 | async-start | bytes 1966080 | tf_op jit(solution)/shard_map/all_to_all | solution.py:333

commit v3 on v2

--- a/solution.py
+++ b/solution.py
@@ -96,11 +96,12 @@
                 keys,
                 (((1,), (1,)), ((), ())),
                 preferred_element_type=F32,
-            ) * (1.0 / math.sqrt(HD))
+            )
             scores = jnp.where(allowed, scores, -1e30)
-            raised = jnp.exp(scores - jnp.max(scores, axis=1, keepdims=True))
+            scores = scores - jnp.max(scores, axis=1, keepdims=True)
+            raised = jnp.exp2(scores * (math.log2(math.e) / math.sqrt(HD)))
             share = 1.0 / jnp.sum(raised, axis=1, keepdims=True)
-            mixed = jnp.dot((raised * share).astype(BF16), values, preferred_element_type=F32)
+            mixed = jnp.dot(raised.astype(BF16), values, preferred_element_type=F32) * share
             out_ref[first:span, cols] = mixed.astype(BF16)
 
 
@@ -339,7 +340,7 @@
     far_up, far_low = shift(behind_up, 1), shift(ahead_low, -1)
     beside = [behind, swap(behind), ahead, swap(ahead)]
     *begun, gate, up = hidden_units(beside, (-1, 1), (w_gate[0], w_up[0], router))
-    (far,) = call(join_kernel, (far_up, far_low), [full], "join", (begun[2],))
+    (far,) = call(join_kernel, (far_up, far_low), [full], "join", (begun[2], down[2]))
     weights = (gate, up, router)
     begun = hidden_units([here, swap(here)], (0,), weights, begun, after=(far,))
     (hidden,) = hidden_units([far, swap(far)], (2,), weights, begun, end=True)

time: 175 us -> 176 us (level)
    unnamed x38 -> x34, local copies, waits for them, and re-layouts: 9.59 us -> 10 us
where the time goes in v3:
time: 176 us; the launch traced here: 175 us
  waiting for transfers between devices  75.1 us (43%)
  Pallas kernels  35.3 us (20%)
  starting transfers between devices  30 us (17%)
  blocking collectives  22.3 us (13%)
  local copies, waits for them, and re-layouts  10.2 us (6%)
    ppermute x16, waiting for transfers between devices, shift(): return lax.ppermute(x, 'x', [(i, (i + by) % size) for i in range(size)])  53.6 us
    pallas_call x16, Pallas kernels, call(): pl.pallas_call(kernel, in_specs=[VMEM] * len(inputs) + [ANY] * len(after)...  29.6 us
    ppermute x16, starting transfers between devices, shift(): return lax.ppermute(x, 'x', [(i, (i + by) % size) for i in range(size)])  23.3 us
    all_to_all x1, blocking collectives, exchange(): lax.all_to_all(x, 'dp', split_axis=0, concat_axis=0, tiled=True)  22.3 us
    all_to_all x1, waiting for transfers between devices, exchange(): lax.all_to_all(x, 'dp', split_axis=0, concat_axis=0, tiled=True)  16.5 us
    unnamed x34, local copies, waits for them, and re-layouts  10 us
    ppermute x10, waiting for transfers between devices, swap(): return lax.ppermute(x, 'c', [(0, 1), (1, 0)])  5.02 us
    all_to_all x1, starting transfers between devices, exchange(): lax.all_to_all(x, 'dp', split_axis=0, concat_axis=0, tiled=True)  3.64 us
  transfers between devices with their start and end apart: 27, of which 11 were waited for; matrix products, arithmetic and copies ran while one was open for 1% of the time, Pallas kernels for 17%

profile of v3, /device:TPU:0, one launch (start us, length us, event | category | flops | bytes accessed | tf_op | source)
XLA Modules:
  0.0 175.1 jit_solution(9009615279452899995)
XLA Ops:
  0.6 2.9 %copy-done = bf16[640,5120]{1,0:T(8,128)(2,1)S(1)} copy-done((bf16[640,5120]{1,0:T(8,128)(2,1)S(1)}, bf16[640,5120]{1,0:T(8,128)(2,1)}, u32[]{:S(2)}) %copy-start) | copy-done | bytes 6553624
  3.5 1.0 columns.2
  5.1 3.1 %attend.1.x_ref = bf16[512,640]{1,0:T(8,128)(2,1)S(1)} custom-call(s32[8,16]{1,0:T(8,128)S(1)} %bitcast.25, bf16[512,640]{1,0:T(8,128)(2,1)S(1)} %copy-done.5, bf16[512,128]{1,0:T(8,128)(2,1)S(1)} %copy-done.9, bf16[512,128]{1,0:T(8,128)(2,1)S(1)} %copy-done.10, f32[8,128]{1,0:T(8,128)S(1)} %get-tuple-element.44.after_ref), custom_call_target="tpu_custom_call" | custom-call | flops 1024 | bytes 1024 | tf_op jit(solution)/shard_map/attend/pallas_call | solution.py:109
  8.4 3.0 %collective-permute-done.xs_ref = bf16[512,640]{1,0:T(8,128)(2,1)S(1)} collective-permute-done((bf16[512,640]{1,0:T(8,128)(2,1)S(1)}, bf16[512,640]{1,0:T(8,128)(2,1)S(1)}, u32[]{:S(2)}, u32[]{:S(2)}) %collective-permute-start) | collective-permute-done | bytes 655392 | tf_op jit(solution)/shard_map/ppermute | solution.py:186
  11.4 1.3 far_blocks.2
  12.7 1.6 collective-permute-start.4
  14.3 1.7 collective-permute-start.5
  16.0 1.3 near_blocks.2
  17.8 2.5 %rest_blocks.2 = (f32[256,640]{1,0:T(8,128)S(1)}, f32[256,640]{1,0:T(8,128)S(1)}, f32[512,640]{1,0:T(8,128)S(1)}) custom-call(bf16[512,640]{1,0:T(8,128)(2,1)S(1)} %attend.1.x_ref, bf16[512,640]{1,0:T(8,128)(2,1)S(1)} %collective-permute-done.xs_ref, bf16[3,640,640]{2,1,0:T(8,128)(2,1)S(1)} %get-tuple-element.45.w_ref, ...), custom_call_target="tpu_custom_call" | custom-call | flops 1024 | bytes 1024 | tf_op jit(solution)/shard_map/rest_blocks/pallas_call | solution.py:174
  20.3 4.3 %collective-permute-done.4.far_up = bf16[256,640]{1,0:T(8,128)(2,1)S(1)} collective-permute-done((bf16[256,640]{1,0:T(8,128)(2,1)S(1)}, bf16[256,640]{1,0:T(8,128)(2,1)S(1)}, u32[]{:S(2)}, u32[]{:S(2)}) %collective-permute-start.4) | collective-permute-done | bytes 327712 | tf_op jit(solution)/shard_map/ppermute | solution.py:191
  24.7 0.8 collective-permute-start.6
  25.5 2.5 %collective-permute-start.8 = (bf16[256,640]{1,0:T(8,128)(2,1)S(1)}, bf16[256,640]{1,0:T(8,128)(2,1)S(1)}, u32[]{:S(2)}, u32[]{:S(2)}) collective-permute-start(bf16[256,640]{1,0:T(8,128)(2,1)S(1)} %get-tuple-element.57), channel_id=1, source_target_pairs={{0,6},{2,0},{4,2},{6,4},{1,7},{3,1},{5,3},{7,5},{8,14},{10,8},{12,... | collective-permute-start | bytes 983048 | tf_op jit(solution)/shard_map/ppermute | solution.py:191
  28.0 0.9 collective-permute-start.3
  29.2 1.7 columns.3
  30.9 1.3 copy-done.12
  32.2 5.6 %collective-permute-done.6.refs_1_ = bf16[256,640]{1,0:T(8,128)(2,1)S(1)} collective-permute-done((bf16[256,640]{1,0:T(8,128)(2,1)S(1)}, bf16[256,640]{1,0:T(8,128)(2,1)S(1)}, u32[]{:S(2)}, u32[]{:S(2)}) %collective-permute-start.6) | collective-permute-done | bytes 327712 | tf_op jit(solution)/shard_map/ppermute | solution.py:191
  37.8 3.1 %collective-permute-done.3.refs_0_ = bf16[256,640]{1,0:T(8,128)(2,1)S(1)} collective-permute-done((bf16[256,640]{1,0:T(8,128)(2,1)S(1)}, bf16[256,640]{1,0:T(8,128)(2,1)S(1)}, u32[]{:S(2)}, u32[]{:S(2)}) %collective-permute-start.3) | collective-permute-done | bytes 327712 | tf_op jit(solution)/shard_map/ppermute | solution.py:191
  40.8 1.4 own_block.2
  42.2 22.3 %all_to_all.10 = bf16[16,48,640]{2,1,0:T(8,128)(2,1)S(1)} all-to-all(bf16[16,48,640]{2,1,0:T(8,128)(2,1)S(1)} %bitcast.22), channel_id=1, replica_groups=mesh['dp'=16,'x'=4,'c'=2] {'dp'}, dimensions={0} | all-to-all | bytes 1966080 | tf_op jit(solution)/shard_map/all_to_all | solution.py:334
  64.5 1.2 collective-permute-start.9
  65.7 2.0 %collective-permute-start.10 = (bf16[768,640]{1,0:T(8,128)(2,1)S(1)}, bf16[768,640]{1,0:T(8,128)(2,1)}, u32[]{:S(2)}, u32[]{:S(2)}) collective-permute-start(bf16[768,640]{1,0:T(8,128)(2,1)S(1)} %bitcast.19), channel_id=1, source_target_pairs={{0,6},{2,0},{4,2},{6,4},{1,7},{3,1},{5,3},{7,5},{8,14},{10,8},{12,... | collective-permute-start | bytes 2949128 | tf_op jit(solution)/shard_map/ppermute | solution.py:191
  67.8 18.0 %collective-permute-done.9.behind_ref.refs_0_ = bf16[768,640]{1,0:T(8,128)(2,1)S(1)} collective-permute-done((bf16[768,640]{1,0:T(8,128)(2,1)S(1)}, bf16[768,640]{1,0:T(8,128)(2,1)S(1)}, u32[]{:S(2)}, u32[]{:S(2)}) %collective-permute-start.9) | collective-permute-done | bytes 983072 | tf_op jit(solution)/shard_map/ppermute | solution.py:191
  86.3 1.3 halves.1
  87.6 1.5 collective-permute-start.11
  89.1 1.8 %collective-permute-start.12 = (bf16[384,640]{1,0:T(8,128)(2,1)S(1)}, bf16[384,640]{1,0:T(8,128)(2,1)S(1)}, u32[]{:S(2)}, u32[]{:S(2)}) collective-permute-start(bf16[384,640]{1,0:T(8,128)(2,1)S(1)} %get-tuple-element.62), channel_id=1, source_target_pairs={{0,6},{2,0},{4,2},{6,4},{1,7},{3,1},{5,3},{7,5},{8,14},{10,8},{12,... | collective-permute-start | bytes 1474568 | tf_op jit(solution)/shard_map/ppermute | solution.py:191
  90.9 0.9 fusion.1.refs_6_.refs_4_
  92.0 2.5 %copy-done.1 = bf16[1,5120,512]{2,1,0:T(8,128)(2,1)S(1)} copy-done((bf16[1,5120,512]{2,1,0:T(8,128)(2,1)S(1)}, bf16[1,5120,512]{2,1,0:T(8,128)(2,1)}, u32[]{:S(2)}) %copy-start.1) | copy-done | bytes 5242904
  94.4 2.5 %copy-done.2 = bf16[1,5120,512]{2,1,0:T(8,128)(2,1)S(1)} copy-done((bf16[1,5120,512]{2,1,0:T(8,128)(2,1)S(1)}, bf16[1,5120,512]{2,1,0:T(8,128)(2,1)}, u32[]{:S(2)}) %copy-start.2) | copy-done | bytes 5242904
  96.9 6.7 %hidden.3 = (f32[768,512]{1,0:T(8,128)S(1)}, f32[768,512]{1,0:T(8,128)S(1)}, f32[768,1]{1,0:T(8,128)S(1)}, f32[768,1]{1,0:T(8,128)S(1)}, bf16[2560,512]{1,0:T(8,128)(2,1)S(1)}, /*index=5*/bf16[2560,512]{1,0:T(8,128)(2,1)S(1)}) custom-call(bf16[768,640]{1,0:T(8,128)(2,1)S(1)} %collective-permute-done.9.behind_ref.refs_0_, ...), custom_call_target="tpu_custom_call" | custom-call | flops 1024 | bytes 1024 | tf_op jit(solution)/shard_map/hidden/pallas_call | solution.py:174
  103.8 0.6 collective-permute-start.16
  104.4 0.8 copy-done.13
  105.7 2.6 %hidden.4 = (f32[768,512]{1,0:T(8,128)S(1)}, f32[768,512]{1,0:T(8,128)S(1)}, f32[768,1]{1,0:T(8,128)S(1)}, f32[768,1]{1,0:T(8,128)S(1)}) custom-call(bf16[768,640]{1,0:T(8,128)(2,1)S(1)} %bitcast.21, bf16[768,640]{1,0:T(8,128)(2,1)S(1)} %collective-permute-done.17.refs_1_, bf16[2560,512]{1,0:T(8,128)(2,1)S(1)} %get-tuple-element.65.refs_2_, ...), custom_call_target="tpu_custom_call" | custom-call | flops 1024 | bytes 1024 | tf_op jit(solution)/shard_map/hidden/pallas_call | solution.py:174
  108.3 2.7 %hidden.5.x_ref = bf16[768,512]{1,0:T(8,128)(2,1)S(1)} custom-call(bf16[768,640]{1,0:T(8,128)(2,1)S(1)} %join.1.refs_9_.refs_0_, bf16[768,640]{1,0:T(8,128)(2,1)S(1)} %collective-permute-done.16.refs_1_, bf16[2560,512]{1,0:T(8,128)(2,1)S(1)} %get-tuple-element.65.refs_2_, bf16[2560,512]{1,0:T(8,128)(2,1)S(1)} %get-tuple-element.66.refs_3_, ...), custom_call_target="tpu_custom_call" | custom-call | flops 1024 | bytes 1024 | tf_op jit(solution)/shard_map/hidden/pallas_call | solution.py:174
  111.5 2.0 %collective-permute-done.18.xs_ref = bf16[768,512]{1,0:T(8,128)(2,1)S(1)} collective-permute-done((bf16[768,512]{1,0:T(8,128)(2,1)S(1)}, bf16[768,512]{1,0:T(8,128)(2,1)S(1)}, u32[]{:S(2)}, u32[]{:S(2)}) %collective-permute-start.18) | collective-permute-done | bytes 786464 | tf_op jit(solution)/shard_map/ppermute | solution.py:186
  113.6 2.5 %far_blocks.3 = (bf16[384,640]{1,0:T(8,128)(2,1)S(1)}, bf16[384,640]{1,0:T(8,128)(2,1)S(1)}) custom-call(bf16[768,512]{1,0:T(8,128)(2,1)S(1)} %hidden.5.x_ref, bf16[768,512]{1,0:T(8,128)(2,1)S(1)} %collective-permute-done.18.xs_ref, bf16[1,512,640]{2,1,0:T(8,128)(2,1)S(1)} %copy-done.8, bf16[1,512,640]{2,1,0:T(8,128)(2,1)} %collective-permute-done.15.refs_1_.ws_ref), custom_call_target="tpu_custom_call" | custom-call | flops 1024 | bytes 1024 | tf_op jit(solution)/shard_map/far_blocks/pallas_call | solution.py:174
  116.3 3.0 %collective-permute-start.22 = (bf16[384,640]{1,0:T(8,128)(2,1)S(1)}, bf16[384,640]{1,0:T(8,128)(2,1)S(1)}, u32[]{:S(2)}, u32[]{:S(2)}) collective-permute-start(bf16[384,640]{1,0:T(8,128)(2,1)S(1)} %get-tuple-element.83), channel_id=1, source_target_pairs={{0,6},{2,0},{4,2},{6,4},{1,7},{3,1},{5,3},{7,5},{8,14},{10,8},{12,... | collective-permute-start | bytes 1474568 | tf_op jit(solution)/shard_map/ppermute | solution.py:191
  119.4 1.4 near_blocks.3
  120.7 0.6 collective-permute-start.20
  121.3 1.5 collective-permute-start.24
  122.8 2.6 %rest_blocks.3 = (f32[384,640]{1,0:T(8,128)S(1)}, f32[384,640]{1,0:T(8,128)S(1)}, f32[768,640]{1,0:T(8,128)S(1)}) custom-call(bf16[768,512]{1,0:T(8,128)(2,1)S(1)} %hidden.5.x_ref, bf16[768,512]{1,0:T(8,128)(2,1)S(1)} %collective-permute-done.18.xs_ref, bf16[3,512,640]{2,1,0:T(8,128)(2,1)S(1)} %get-tuple-element.74.w_ref, ...), custom_call_target="tpu_custom_call" | custom-call | flops 1024 | bytes 1024 | tf_op jit(solution)/shard_map/rest_blocks/pallas_call | solution.py:174
  125.4 5.9 %collective-permute-done.21.far_up = bf16[384,640]{1,0:T(8,128)(2,1)S(1)} collective-permute-done((bf16[384,640]{1,0:T(8,128)(2,1)S(1)}, bf16[384,640]{1,0:T(8,128)(2,1)S(1)}, u32[]{:S(2)}, u32[]{:S(2)}) %collective-permute-start.21) | collective-permute-done | bytes 491552 | tf_op jit(solution)/shard_map/ppermute | solution.py:191
  131.8 3.1 %collective-permute-start.25 = (bf16[384,640]{1,0:T(8,128)(2,1)S(1)}, bf16[384,640]{1,0:T(8,128)(2,1)S(1)}, u32[]{:S(2)}, u32[]{:S(2)}) collective-permute-start(bf16[384,640]{1,0:T(8,128)(2,1)S(1)} %get-tuple-element.85), channel_id=1, source_target_pairs={{0,6},{2,0},{4,2},{6,4},{1,7},{3,1},{5,3},{7,5},{8,14},{10,8},{12,... | collective-permute-start | bytes 1474568 | tf_op jit(solution)/shard_map/ppermute | solution.py:191
  135.0 6.5 %collective-permute-done.20.refs_0_ = bf16[384,640]{1,0:T(8,128)(2,1)S(1)} collective-permute-done((bf16[384,640]{1,0:T(8,128)(2,1)S(1)}, bf16[384,640]{1,0:T(8,128)(2,1)S(1)}, u32[]{:S(2)}, u32[]{:S(2)}) %collective-permute-start.20) | collective-permute-done | bytes 491552 | tf_op jit(solution)/shard_map/ppermute | solution.py:191
  141.9 9.8 %collective-permute-done.23.refs_1_ = bf16[384,640]{1,0:T(8,128)(2,1)S(1)} collective-permute-done((bf16[384,640]{1,0:T(8,128)(2,1)S(1)}, bf16[384,640]{1,0:T(8,128)(2,1)S(1)}, u32[]{:S(2)}, u32[]{:S(2)}) %collective-permute-start.23) | collective-permute-done | bytes 491552 | tf_op jit(solution)/shard_map/ppermute | solution.py:191
  151.8 1.3 own_block.3
  153.0 3.6 %all-to-all-start.1 = ((bf16[16,48,640]{2,1,0:T(8,128)(2,1)}), bf16[16,48,640]{2,1,0:T(8,128)(2,1)S(1)}, u32[]{:S(2)}, u32[]{:S(2)}) async-start(bf16[16,48,640]{2,1,0:T(8,128)(2,1)} %bitcast.9), calls=%async_computation.1 | async-start | bytes 1966080 | tf_op jit(solution)/shard_map/all_to_all | solution.py:334
  156.8 16.5 %all-to-all-done.1 = bf16[16,48,640]{2,1,0:T(8,128)(2,1)S(1)} async-done(((bf16[16,48,640]{2,1,0:T(8,128)(2,1)}), bf16[16,48,640]{2,1,0:T(8,128)(2,1)S(1)}, u32[]{:S(2)}, u32[]{:S(2)}) %all-to-all-start.1) | async-done | bytes 983072 | tf_op jit(solution)/shard_map/all_to_all | solution.py:334
  173.4 1.7 from_slots.1
  (65 shorter events, 4.7 us)
Async XLA Ops:
  0.6 2.9 %copy-start = (bf16[640,5120]{1,0:T(8,128)(2,1)S(1)}, bf16[640,5120]{1,0:T(8,128)(2,1)}, u32[]{:S(2)}) copy-start(bf16[640,5120]{1,0:T(8,128)(2,1)} %w_ref.1) | copy-start | bytes 19660804
  3.5 1.6 copy-start.5
  3.5 1.6 copy-start.9
  3.5 1.6 copy-start.10
  3.5 1.6 copy-start.11
  4.5 11.5 %collective-permute-start.1 = (bf16[3,640,640]{2,1,0:T(8,128)(2,1)S(1)}, bf16[3,640,640]{2,1,0:T(8,128)(2,1)S(1)}, u32[]{:S(2)}, u32[]{:S(2)}) collective-permute-start(bf16[3,640,640]{2,1,0:T(8,128)(2,1)S(1)} %get-tuple-element.46), channel_id=1, source_target_pairs={{0,1},{1,0},{2,3},{3,2},{4,5},{5,4},{6,7},{7,6},{8,9},{9,8},{10,11... | collective-permute-start | bytes 7372808 | tf_op jit(solution)/shard_map/ppermute | solution.py:186
  4.6 6.8 %collective-permute-start.2 = (bf16[1,640,640]{2,1,0:T(8,128)(2,1)S(1)}, bf16[1,640,640]{2,1,0:T(8,128)(2,1)S(1)}, u32[]{:S(2)}, u32[]{:S(2)}) collective-permute-start(bf16[1,640,640]{2,1,0:T(8,128)(2,1)S(1)} %get-tuple-element.48), channel_id=1, source_target_pairs={{0,1},{1,0},{2,3},{3,2},{4,5},{5,4},{6,7},{7,6},{8,9},{9,8},{10,11... | collective-permute-start | bytes 2457608 | tf_op jit(solution)/shard_map/ppermute | solution.py:186
  8.2 3.1 %collective-permute-start = (bf16[512,640]{1,0:T(8,128)(2,1)S(1)}, bf16[512,640]{1,0:T(8,128)(2,1)S(1)}, u32[]{:S(2)}, u32[]{:S(2)}) collective-permute-start(bf16[512,640]{1,0:T(8,128)(2,1)S(1)} %attend.1.x_ref), channel_id=1, source_target_pairs={{0,1},{1,0},{2,3},{3,2},{4,5},{5,4},{6,7},{7,6},{8,9},{9,8},{10,11... | collective-permute-start | bytes 1966088 | tf_op jit(solution)/shard_map/ppermute | solution.py:186
  12.7 11.8 %collective-permute-start.4 = (bf16[256,640]{1,0:T(8,128)(2,1)S(1)}, bf16[256,640]{1,0:T(8,128)(2,1)S(1)}, u32[]{:S(2)}, u32[]{:S(2)}) collective-permute-start(bf16[256,640]{1,0:T(8,128)(2,1)S(1)} %get-tuple-element.49.after_ref), channel_id=1, source_target_pairs={{0,2},{2,4},{4,6},{6,0},{1,3},{3,5},{5,7},{7,1},{8,10},{10,12},{12... | collective-permute-start | bytes 983048 | tf_op jit(solution)/shard_map/ppermute | solution.py:191
  14.3 10.2 %collective-permute-start.5 = (bf16[256,640]{1,0:T(8,128)(2,1)S(1)}, bf16[256,640]{1,0:T(8,128)(2,1)S(1)}, u32[]{:S(2)}, u32[]{:S(2)}) collective-permute-start(bf16[256,640]{1,0:T(8,128)(2,1)S(1)} %get-tuple-element.55), channel_id=1, source_target_pairs={{0,6},{2,0},{4,2},{6,4},{1,7},{3,1},{5,3},{7,5},{8,14},{10,8},{12,... | collective-permute-start | bytes 983048 | tf_op jit(solution)/shard_map/ppermute | solution.py:191
  16.0 13.2 %slice-start = ((s8[5242880]{0:T(1024)(128)(4,1)}), s8[4194304]{0:T(1024)(128)(4,1)S(1)}, s32[]{:S(2)}) async-start(s8[5242880]{0:T(1024)(128)(4,1)} %bitcast.14), calls=%async_computation.2 | async-start | bytes 8388608
  17.3 11.6 %copy-start.14 = (s32[512]{0:T(512)S(1)}, s32[512]{0:T(512)}, u32[]{:S(2)}) copy-start(s32[512]{0:T(512)} %param.18) | copy-start | bytes 6148
  17.3 11.8 %slice-start.1 = ((s8[5242880]{0:T(1024)(128)(4,1)}), s8[1048576]{0:T(1024)(128)(4,1)S(1)}, s32[]{:S(2)}) async-start(s8[5242880]{0:T(1024)(128)(4,1)} %bitcast.14), calls=%async_computation.3 | async-start | bytes 2097152
  17.4 20.4 %collective-permute-start.7 = (bf16[256,640]{1,0:T(8,128)(2,1)S(1)}, bf16[256,640]{1,0:T(8,128)(2,1)S(1)}, u32[]{:S(2)}, u32[]{:S(2)}) collective-permute-start(bf16[256,640]{1,0:T(8,128)(2,1)S(1)} %get-tuple-element.50.after_ref), channel_id=1, source_target_pairs={{0,2},{2,4},{4,6},{6,0},{1,3},{3,5},{5,7},{7,1},{8,10},{10,12},{12... | collective-permute-start | bytes 983048 | tf_op jit(solution)/shard_map/ppermute | solution.py:191
  24.7 13.1 %collective-permute-start.6 = (bf16[256,640]{1,0:T(8,128)(2,1)S(1)}, bf16[256,640]{1,0:T(8,128)(2,1)S(1)}, u32[]{:S(2)}, u32[]{:S(2)}) collective-permute-start(bf16[256,640]{1,0:T(8,128)(2,1)S(1)} %get-tuple-element.56.refs_0_), channel_id=1, source_target_pairs={{0,2},{2,4},{4,6},{6,0},{1,3},{3,5},{5,7},{7,1},{8,10},{10,12},{12... | collective-permute-start | bytes 983048 | tf_op jit(solution)/shard_map/ppermute | solution.py:191
  25.5 12.3 %collective-permute-start.8 = (bf16[256,640]{1,0:T(8,128)(2,1)S(1)}, bf16[256,640]{1,0:T(8,128)(2,1)S(1)}, u32[]{:S(2)}, u32[]{:S(2)}) collective-permute-start(bf16[256,640]{1,0:T(8,128)(2,1)S(1)} %get-tuple-element.57), channel_id=1, source_target_pairs={{0,6},{2,0},{4,2},{6,4},{1,7},{3,1},{5,3},{7,5},{8,14},{10,8},{12,... | collective-permute-start | bytes 983048 | tf_op jit(solution)/shard_map/ppermute | solution.py:191
  28.0 12.9 %collective-permute-start.3 = (bf16[256,640]{1,0:T(8,128)(2,1)S(1)}, bf16[256,640]{1,0:T(8,128)(2,1)S(1)}, u32[]{:S(2)}, u32[]{:S(2)}) collective-permute-start(bf16[256,640]{1,0:T(8,128)(2,1)S(1)} %get-tuple-element.52), channel_id=1, source_target_pairs={{0,6},{2,0},{4,2},{6,4},{1,7},{3,1},{5,3},{7,5},{8,14},{10,8},{12,... | collective-permute-start | bytes 983048 | tf_op jit(solution)/shard_map/ppermute | solution.py:191
  29.2 11.6 %copy-start.6 = (bf16[512,640]{1,0:T(8,128)(2,1)S(1)}, bf16[512,640]{1,0:T(8,128)(2,1)}, u32[]{:S(2)}) copy-start(bf16[512,640]{1,0:T(8,128)(2,1)} %refs_4_.1) | copy-start | bytes 1966084
  30.9 1.3 copy-start.12
  32.2 32.3 %copy-start.7 = (bf16[1,512,640]{2,1,0:T(8,128)(2,1)}, bf16[1,512,640]{2,1,0:T(8,128)(2,1)S(1)}, u32[]{:S(2)}) copy-start(bf16[1,512,640]{2,1,0:T(8,128)(2,1)S(1)} %get-tuple-element.76.w_ref) | copy-start | bytes 1966084
  64.5 21.2 %copy-start.3 = (bf16[16,48,640]{2,1,0:T(8,128)(2,1)}, bf16[16,48,640]{2,1,0:T(8,128)(2,1)S(1)}, u32[]{:S(2)}) copy-start(bf16[16,48,640]{2,1,0:T(8,128)(2,1)S(1)} %all_to_all.10) | copy-start | bytes 2949124
  64.5 21.2 %collective-permute-start.9 = (bf16[768,640]{1,0:T(8,128)(2,1)S(1)}, bf16[768,640]{1,0:T(8,128)(2,1)S(1)}, u32[]{:S(2)}, u32[]{:S(2)}) collective-permute-start(bf16[768,640]{1,0:T(8,128)(2,1)S(1)} %bitcast.18), channel_id=1, source_target_pairs={{0,2},{2,4},{4,6},{6,0},{1,3},{3,5},{5,7},{7,1},{8,10},{10,12},{12... | collective-permute-start | bytes 2949128 | tf_op jit(solution)/shard_map/ppermute | solution.py:191
  65.7 20.0 %collective-permute-start.10 = (bf16[768,640]{1,0:T(8,128)(2,1)S(1)}, bf16[768,640]{1,0:T(8,128)(2,1)}, u32[]{:S(2)}, u32[]{:S(2)}) collective-permute-start(bf16[768,640]{1,0:T(8,128)(2,1)S(1)} %bitcast.19), channel_id=1, source_target_pairs={{0,6},{2,0},{4,2},{6,4},{1,7},{3,1},{5,3},{7,5},{8,14},{10,8},{12,... | collective-permute-start | bytes 2949128 | tf_op jit(solution)/shard_map/ppermute | solution.py:191
  85.7 6.1 %collective-permute-start.13 = (bf16[768,640]{1,0:T(8,128)(2,1)S(1)}, bf16[768,640]{1,0:T(8,128)(2,1)}, u32[]{:S(2)}, u32[]{:S(2)}) collective-permute-start(bf16[768,640]{1,0:T(8,128)(2,1)S(1)} %collective-permute-done.9.behind_ref.refs_0_), channel_id=1, source_target_pairs={{0,1},{1,0},{2,3},{3,2},{4,5},{5,4},{6,7},{7,6},{8,9},{9,8},{10,11... | collective-permute-start | bytes 2949128 | tf_op jit(solution)/shard_map/ppermute | solution.py:186
  85.7 6.2 %collective-permute-start.14 = (bf16[768,640]{1,0:T(8,128)(2,1)}, bf16[768,640]{1,0:T(8,128)(2,1)}, u32[]{:S(2)}, u32[]{:S(2)}) collective-permute-start(bf16[768,640]{1,0:T(8,128)(2,1)} %collective-permute-done.10.ahead_ref.refs_2_), channel_id=1, source_target_pairs={{0,1},{1,0},{2,3},{3,2},{4,5},{5,4},{6,7},{7,6},{8,9},{9,8},{10,11... | collective-permute-start | bytes 2949128 | tf_op jit(solution)/shard_map/ppermute | solution.py:186
  86.2 17.4 %collective-permute-start.15 = (bf16[1,512,640]{2,1,0:T(8,128)(2,1)}, bf16[1,512,640]{2,1,0:T(8,128)(2,1)}, u32[]{:S(2)}, u32[]{:S(2)}) collective-permute-start(bf16[1,512,640]{2,1,0:T(8,128)(2,1)} %get-tuple-element.64), channel_id=1, source_target_pairs={{0,1},{1,0},{2,3},{3,2},{4,5},{5,4},{6,7},{7,6},{8,9},{9,8},{10,11... | collective-permute-start | bytes 1966088 | tf_op jit(solution)/shard_map/ppermute | solution.py:186
  87.6 16.1 %collective-permute-start.11 = (bf16[384,640]{1,0:T(8,128)(2,1)S(1)}, bf16[384,640]{1,0:T(8,128)(2,1)S(1)}, u32[]{:S(2)}, u32[]{:S(2)}) collective-permute-start(bf16[384,640]{1,0:T(8,128)(2,1)S(1)} %get-tuple-element.61), channel_id=1, source_target_pairs={{0,2},{2,4},{4,6},{6,0},{1,3},{3,5},{5,7},{7,1},{8,10},{10,12},{12... | collective-permute-start | bytes 1474568 | tf_op jit(solution)/shard_map/ppermute | solution.py:191
  89.1 14.6 %collective-permute-start.12 = (bf16[384,640]{1,0:T(8,128)(2,1)S(1)}, bf16[384,640]{1,0:T(8,128)(2,1)S(1)}, u32[]{:S(2)}, u32[]{:S(2)}) collective-permute-start(bf16[384,640]{1,0:T(8,128)(2,1)S(1)} %get-tuple-element.62), channel_id=1, source_target_pairs={{0,6},{2,0},{4,2},{6,4},{1,7},{3,1},{5,3},{7,5},{8,14},{10,8},{12,... | collective-permute-start | bytes 1474568 | tf_op jit(solution)/shard_map/ppermute | solution.py:191
  91.8 13.9 %collective-permute-start.17 = (bf16[768,640]{1,0:T(8,128)(2,1)}, bf16[768,640]{1,0:T(8,128)(2,1)S(1)}, u32[]{:S(2)}, u32[]{:S(2)}) collective-permute-start(bf16[768,640]{1,0:T(8,128)(2,1)} %bitcast.20), channel_id=1, source_target_pairs={{0,1},{1,0},{2,3},{3,2},{4,5},{5,4},{6,7},{7,6},{8,9},{9,8},{10,11... | collective-permute-start | bytes 2949128 | tf_op jit(solution)/shard_map/ppermute | solution.py:186
  91.9 2.5 %copy-start.1 = (bf16[1,5120,512]{2,1,0:T(8,128)(2,1)S(1)}, bf16[1,5120,512]{2,1,0:T(8,128)(2,1)}, u32[]{:S(2)}) copy-start(bf16[1,5120,512]{2,1,0:T(8,128)(2,1)} %param.19) | copy-start | bytes 15728644
  94.4 2.5 %copy-start.2 = (bf16[1,5120,512]{2,1,0:T(8,128)(2,1)S(1)}, bf16[1,5120,512]{2,1,0:T(8,128)(2,1)}, u32[]{:S(2)}) copy-start(bf16[1,5120,512]{2,1,0:T(8,128)(2,1)} %param.20) | copy-start | bytes 15728644
  103.6 1.5 copy-start.13
  103.7 2.0 %copy-start.4 = (bf16[16,48,640]{2,1,0:T(8,128)(2,1)S(1)}, bf16[16,48,640]{2,1,0:T(8,128)(2,1)}, u32[]{:S(2)}) copy-start(bf16[16,48,640]{2,1,0:T(8,128)(2,1)} %copy-done.3) | copy-start | bytes 2949124
  103.8 4.5 %collective-permute-start.16 = (bf16[768,640]{1,0:T(8,128)(2,1)S(1)}, bf16[768,640]{1,0:T(8,128)(2,1)S(1)}, u32[]{:S(2)}, u32[]{:S(2)}) collective-permute-start(bf16[768,640]{1,0:T(8,128)(2,1)S(1)} %join.1.refs_9_.refs_0_), channel_id=1, source_target_pairs={{0,1},{1,0},{2,3},{3,2},{4,5},{5,4},{6,7},{7,6},{8,9},{9,8},{10,11... | collective-permute-start | bytes 2949128 | tf_op jit(solution)/shard_map/ppermute | solution.py:186
  105.2 14.2 %collective-permute-start.19 = (bf16[3,512,640]{2,1,0:T(8,128)(2,1)S(1)}, bf16[3,512,640]{2,1,0:T(8,128)(2,1)S(1)}, u32[]{:S(2)}, u32[]{:S(2)}) collective-permute-start(bf16[3,512,640]{2,1,0:T(8,128)(2,1)S(1)} %copy-done.13), channel_id=1, source_target_pairs={{0,1},{1,0},{2,3},{3,2},{4,5},{5,4},{6,7},{7,6},{8,9},{9,8},{10,11... | collective-permute-start | bytes 5898248 | tf_op jit(solution)/shard_map/ppermute | solution.py:186
  108.3 5.3 %copy-start.8 = (bf16[1,512,640]{2,1,0:T(8,128)(2,1)S(1)}, bf16[1,512,640]{2,1,0:T(8,128)(2,1)}, u32[]{:S(2)}) copy-start(bf16[1,512,640]{2,1,0:T(8,128)(2,1)} %copy-done.7) | copy-start | bytes 1966084
  111.0 2.6 %collective-permute-start.18 = (bf16[768,512]{1,0:T(8,128)(2,1)S(1)}, bf16[768,512]{1,0:T(8,128)(2,1)S(1)}, u32[]{:S(2)}, u32[]{:S(2)}) collective-permute-start(bf16[768,512]{1,0:T(8,128)(2,1)S(1)} %hidden.5.x_ref), channel_id=1, source_target_pairs={{0,1},{1,0},{2,3},{3,2},{4,5},{5,4},{6,7},{7,6},{8,9},{9,8},{10,11... | collective-permute-start | bytes 2359304 | tf_op jit(solution)/shard_map/ppermute | solution.py:186
  116.0 15.3 %collective-permute-start.21 = (bf16[384,640]{1,0:T(8,128)(2,1)S(1)}, bf16[384,640]{1,0:T(8,128)(2,1)S(1)}, u32[]{:S(2)}, u32[]{:S(2)}) collective-permute-start(bf16[384,640]{1,0:T(8,128)(2,1)S(1)} %get-tuple-element.77.after_ref), channel_id=1, source_target_pairs={{0,2},{2,4},{4,6},{6,0},{1,3},{3,5},{5,7},{7,1},{8,10},{10,12},{12... | collective-permute-start | bytes 1474568 | tf_op jit(solution)/shard_map/ppermute | solution.py:191
  116.3 15.1 %collective-permute-start.22 = (bf16[384,640]{1,0:T(8,128)(2,1)S(1)}, bf16[384,640]{1,0:T(8,128)(2,1)S(1)}, u32[]{:S(2)}, u32[]{:S(2)}) collective-permute-start(bf16[384,640]{1,0:T(8,128)(2,1)S(1)} %get-tuple-element.83), channel_id=1, source_target_pairs={{0,6},{2,0},{4,2},{6,4},{1,7},{3,1},{5,3},{7,5},{8,14},{10,8},{12,... | collective-permute-start | bytes 1474568 | tf_op jit(solution)/shard_map/ppermute | solution.py:191
  120.7 20.8 %collective-permute-start.20 = (bf16[384,640]{1,0:T(8,128)(2,1)S(1)}, bf16[384,640]{1,0:T(8,128)(2,1)S(1)}, u32[]{:S(2)}, u32[]{:S(2)}) collective-permute-start(bf16[384,640]{1,0:T(8,128)(2,1)S(1)} %get-tuple-element.80), channel_id=1, source_target_pairs={{0,6},{2,0},{4,2},{6,4},{1,7},{3,1},{5,3},{7,5},{8,14},{10,8},{12,... | collective-permute-start | bytes 1474568 | tf_op jit(solution)/shard_map/ppermute | solution.py:191
  121.3 20.6 %collective-permute-start.24 = (bf16[384,640]{1,0:T(8,128)(2,1)S(1)}, bf16[384,640]{1,0:T(8,128)(2,1)S(1)}, u32[]{:S(2)}, u32[]{:S(2)}) collective-permute-start(bf16[384,640]{1,0:T(8,128)(2,1)S(1)} %get-tuple-element.78.after_ref), channel_id=1, source_target_pairs={{0,2},{2,4},{4,6},{6,0},{1,3},{3,5},{5,7},{7,1},{8,10},{10,12},{12... | collective-permute-start | bytes 1474568 | tf_op jit(solution)/shard_map/ppermute | solution.py:191
  131.6 20.2 %collective-permute-start.23 = (bf16[384,640]{1,0:T(8,128)(2,1)S(1)}, bf16[384,640]{1,0:T(8,128)(2,1)S(1)}, u32[]{:S(2)}, u32[]{:S(2)}) collective-permute-start(bf16[384,640]{1,0:T(8,128)(2,1)S(1)} %get-tuple-element.84), channel_id=1, source_target_pairs={{0,2},{2,4},{4,6},{6,0},{1,3},{3,5},{5,7},{7,1},{8,10},{10,12},{12... | collective-permute-start | bytes 1474568 | tf_op jit(solution)/shard_map/ppermute | solution.py:191
  131.8 19.9 %collective-permute-start.25 = (bf16[384,640]{1,0:T(8,128)(2,1)S(1)}, bf16[384,640]{1,0:T(8,128)(2,1)S(1)}, u32[]{:S(2)}, u32[]{:S(2)}) collective-permute-start(bf16[384,640]{1,0:T(8,128)(2,1)S(1)} %get-tuple-element.85), channel_id=1, source_target_pairs={{0,6},{2,0},{4,2},{6,4},{1,7},{3,1},{5,3},{7,5},{8,14},{10,8},{12,... | collective-permute-start | bytes 1474568 | tf_op jit(solution)/shard_map/ppermute | solution.py:191
  153.0 20.3 %all-to-all-start.1 = ((bf16[16,48,640]{2,1,0:T(8,128)(2,1)}), bf16[16,48,640]{2,1,0:T(8,128)(2,1)S(1)}, u32[]{:S(2)}, u32[]{:S(2)}) async-start(bf16[16,48,640]{2,1,0:T(8,128)(2,1)} %bitcast.9), calls=%async_computation.1 | async-start | bytes 1966080 | tf_op jit(solution)/shard_map/all_to_all | solution.py:334
